TPU v7x, 32 devices: a whole 2x2x4 slice. The times are simulated.
32 devices in a mesh: dp: 16 (over z, y, x), head: 2 (over core).
Axes of the slice: x: 2, y: 2, z: 4, core: 2. Of those that a mesh axis runs over, the one named last changes fastest.
Arguments:
- tokens: bfloat16 [288, 198, 384], P(('dp', 'head')), may hold values from -6 to 6
- cotangent: bfloat16 [288, 198, 384], P(('dp', 'head')), may hold values from -6 to 6
- keep_mask: int32 [288, 198], P(('dp', 'head')), may hold values from 0 to 1, as said below
- source: int32 [288], P(('dp', 'head')), may hold values from 0 to 95, as said below
- qkv_master: float32 [384, 1152], P('dp'), may hold values from -0.3125 to 0.3125
- proj_master: float32 [384, 384], P('dp'), may hold values from -1.25 to 1.25
- fc1_master: float32 [384, 1536], P('dp'), may hold values from -0.3125 to 0.3125
- fc2_master: float32 [1536, 384], P('dp'), may hold values from -0.15625 to 0.15625
- vec_master: float32 [12, 384], P(None, 'dp'), may hold values from -1.2 to 1.4, as said below
- qkv_first: float32 [384, 1152], P('dp'), may hold values from -160 to 160
- proj_first: float32 [384, 384], P('dp'), may hold values from -24 to 24
- fc1_first: float32 [384, 1536], P('dp'), may hold values from -40 to 40
- fc2_first: float32 [1536, 384], P('dp'), may hold values from -80 to 80
- vec_first: float32 [12, 384], P(None, 'dp'), may hold values from -160 to 160
- qkv_second: float32 [384, 1152], P('dp'), may hold values from 28.512 to 456.192
- proj_second: float32 [384, 384], P('dp'), may hold values from 0.6443712 to 10.26432
- fc1_second: float32 [384, 1536], P('dp'), may hold values from 1.7848512 to 28.512
- fc2_second: float32 [1536, 384], P('dp'), may hold values from 7.128 to 114.048
- vec_second: float32 [12, 384], P(None, 'dp'), may hold values from 28.512 to 456.192
Outputs:
- layer_out: bfloat16 [288, 198, 384], P(('dp', 'head'))
- input_grad: float32 [288, 198, 384], P(('dp', 'head'))
- qkv_first_new: float32 [384, 1152], P('dp')
- qkv_second_new: float32 [384, 1152], P('dp')
- qkv_new: float32 [384, 1152], P('dp')
- proj_first_new: float32 [384, 384], P('dp')
- proj_second_new: float32 [384, 384], P('dp')
- proj_new: float32 [384, 384], P('dp')
- fc1_first_new: float32 [384, 1536], P('dp')
- fc1_second_new: float32 [384, 1536], P('dp')
- fc1_new: float32 [384, 1536], P('dp')
- fc2_first_new: float32 [1536, 384], P('dp')
- fc2_second_new: float32 [1536, 384], P('dp')
- fc2_new: float32 [1536, 384], P('dp')
- vec_first_new: float32 [12, 384], P(None, 'dp')
- vec_second_new: float32 [12, 384], P(None, 'dp')
- vec_new: float32 [12, 384], P(None, 'dp')
Inputs may be any that keep to these rules, and one draw needn't show every extreme that they name: `keep_mask`: 1 keeps a token; tokens 0 and 1 of every image (class and distillation tokens) are always kept. Every source number names exactly three images, and these stand on three different indices of dp. `vec_master`: rows 0 and 5 lie between 0.6 and 1.4.
All inputs are finite; a program needn't handle non-finite values.
Results may differ from a plain program's by a relative error of at most 0.012.
The roundings to bfloat16 on the way count: a program that leaves them out, or rounds other values in their place, can miss the bound.
Values may be sent and summed in bfloat16 or wider, within the bound.
A program may use at most 128 MiB of HBM per device.

v0:
```python
import jax
import jax.numpy as jnp
from jax import lax
from jax.sharding import PartitionSpec as P

HEADS = 6
HEAD_DIM = 64
STEP = 10


norm_eps = 1e-06
step_rates = (0.1, 0.4, 0.1, 0.05, 0.5)
decays = (0.05, 0.05, 0.05, 0.05, 0.0)


def layer_norm(values, gain_row, shift_row):
    average = jnp.mean(values, -1, keepdims=True)
    centred = values - average
    variance = jnp.mean(centred * centred, -1, keepdims=True)
    return centred * lax.rsqrt(variance + norm_eps) * gain_row + shift_row


def gelu_exact(values):
    return jax.nn.gelu(values, approximate=False)


def across(left, right):
    return lax.dot_general(
        left, right, (((0,), (0,)), ((), ())), preferred_element_type=jnp.float32
    )


def against(left, right):
    return lax.dot_general(
        left, right, (((1,), (1,)), ((), ())), preferred_element_type=jnp.float32
    )


def score_block(query_rows, key_rows, key_alive):
    raw_scores = jnp.einsum(
        "ishd,ithd->ihst", query_rows, key_rows, preferred_element_type=jnp.float32
    ) * HEAD_DIM ** (-0.5)
    return jnp.where(key_alive[:, None, None, :], raw_scores, -1000000000.0)


def adamw(master, first, second, gradient, step_rate, weight_decay):
    first_new = 0.9 * first + 0.1 * gradient
    second_new = 0.999 * second + 0.001 * gradient * gradient
    step_size = first_new / (1.0 - 0.9**STEP) / (jnp.sqrt(second_new / (1.0 - 0.999**STEP)) + 1e-08)
    return (first_new, second_new, master - step_rate * (step_size + weight_decay * master))


def on_device(
    tokens,
    cotangent,
    keep_mask,
    source,
    qkv_master,
    proj_master,
    fc1_master,
    fc2_master,
    vec_master,
    qkv_first,
    proj_first,
    fc1_first,
    fc2_first,
    vec_first,
    qkv_second,
    proj_second,
    fc1_second,
    fc2_second,
    vec_second,
):
    groups = lax.axis_size("head")
    w_qkv, w_proj, w_fc1, w_fc2, vec_low = (
        lax.all_gather(qkv_master.astype(jnp.bfloat16), "dp", axis=0, tiled=True),
        lax.all_gather(proj_master.astype(jnp.bfloat16), "dp", axis=0, tiled=True),
        lax.all_gather(fc1_master.astype(jnp.bfloat16), "dp", axis=0, tiled=True),
        lax.all_gather(fc2_master.astype(jnp.bfloat16), "dp", axis=0, tiled=True),
        lax.all_gather(vec_master.astype(jnp.bfloat16), "dp", axis=1, tiled=True),
    )
    vectors = vec_low.astype(jnp.float32)
    images, length_all, features = tokens.shape
    pair_images = images * groups
    row_count = images * length_all
    heads_here = HEADS // groups
    group_width = heads_here * HEAD_DIM
    live_mask = keep_mask.astype(jnp.float32)
    kept_rows = jnp.sum(live_mask, 1)
    total_sources = pair_images * lax.axis_size("dp") // 3
    onehot = (source[:, None] == jnp.arange(total_sources, dtype=jnp.int32)[None, :]).astype(
        jnp.float32
    )
    totals = lax.psum(jnp.sum(onehot * kept_rows[:, None], 0), ("dp", "head"))
    image_total = jnp.sum(onehot * totals[None, :], 1)
    token_weight = live_mask * (length_all / image_total)[:, None]
    inputs = tokens.astype(jnp.float32)
    normed, pull_first = jax.vjp(layer_norm, inputs, vectors[0], vectors[1])
    normed_low = normed.reshape(row_count, features).astype(jnp.bfloat16)
    qkv_bias = jnp.concatenate([vectors[2], jnp.zeros_like(vectors[2]), vectors[3]])
    projected = jnp.dot(normed_low, w_qkv, preferred_element_type=jnp.float32) + qkv_bias
    projected = projected.astype(jnp.bfloat16)
    projected = projected.reshape(images, length_all, 3, groups, group_width)
    live_cols = jnp.broadcast_to(
        keep_mask.astype(jnp.bfloat16)[:, :, None, None, None], (images, length_all, 1, groups, 1)
    )
    mine, live_all = (
        lax.all_to_all(projected, "head", split_axis=3, concat_axis=0, tiled=True),
        lax.all_to_all(live_cols, "head", split_axis=3, concat_axis=0, tiled=True),
    )
    mine = mine.reshape(pair_images, length_all, 3, heads_here, HEAD_DIM)
    key_alive = live_all.reshape(pair_images, length_all) > 0
    query_rows = mine[:, :, 0]
    key_rows = mine[:, :, 1]
    value_rows = mine[:, :, 2]
    attn_images = query_rows.shape[0]
    scores = score_block(query_rows, key_rows, key_alive)
    row_max = jnp.max(scores, -1, keepdims=True)
    exponent = jnp.exp(scores - row_max)
    row_total = jnp.sum(exponent, -1, keepdims=True)
    log_total = row_max + jnp.log(row_total)
    probs_low = (exponent / row_total).astype(jnp.bfloat16)
    attended = jnp.einsum(
        "ihst,ithd->ishd", probs_low, value_rows, preferred_element_type=jnp.float32
    )
    attended = attended.astype(jnp.bfloat16)
    returned = lax.all_to_all(
        attended.reshape(pair_images, length_all, 1, group_width),
        "head",
        split_axis=0,
        concat_axis=2,
        tiled=True,
    )
    merged = returned.reshape(row_count, features)
    middle = inputs + (
        jnp.dot(merged, w_proj, preferred_element_type=jnp.float32) + vectors[4]
    ).reshape(images, length_all, features)
    normed_mid, pull_second = jax.vjp(layer_norm, middle, vectors[5], vectors[6])
    normed_mid_low = normed_mid.reshape(row_count, features).astype(jnp.bfloat16)
    hidden = jnp.dot(normed_mid_low, w_fc1, preferred_element_type=jnp.float32) + vectors[
        8:
    ].reshape(-1)
    active, pull_gelu = jax.vjp(gelu_exact, hidden)
    active_low = active.astype(jnp.bfloat16)
    mlp_out = jnp.dot(active_low, w_fc2, preferred_element_type=jnp.float32) + vectors[7]
    layer_out = (
        (middle.reshape(row_count, features) + mlp_out)
        .astype(jnp.bfloat16)
        .reshape(images, length_all, features)
    )
    grad_out = (cotangent.astype(jnp.float32) * token_weight[:, :, None]).reshape(
        row_count, features
    )
    grad_out_low = grad_out.astype(jnp.bfloat16)
    grad_fc2 = across(active_low, grad_out_low)
    bias_fc2 = jnp.sum(grad_out_low.astype(jnp.float32), 0)
    grad_active = against(grad_out_low, w_fc2)
    grad_hidden_low = pull_gelu(grad_active)[0].astype(jnp.bfloat16)
    grad_fc1 = across(normed_mid_low, grad_hidden_low)
    bias_fc1 = jnp.sum(grad_hidden_low.astype(jnp.float32), 0)
    grad_normed_mid = against(grad_hidden_low, w_fc1).reshape(images, length_all, features)
    grad_mid_norm, gain_second, shift_second = pull_second(grad_normed_mid)
    grad_middle = grad_out + grad_mid_norm.reshape(row_count, features)
    grad_middle_low = grad_middle.astype(jnp.bfloat16)
    grad_proj = across(merged, grad_middle_low)
    bias_proj = jnp.sum(grad_middle_low.astype(jnp.float32), 0)
    grad_merged = against(grad_middle_low, w_proj).astype(jnp.bfloat16)
    grad_attended = lax.all_to_all(
        grad_merged.reshape(images, length_all, groups, group_width),
        "head",
        split_axis=2,
        concat_axis=0,
        tiled=True,
    )
    grad_attended = grad_attended.reshape(pair_images, length_all, heads_here, HEAD_DIM)
    scores_again = score_block(query_rows, key_rows, key_alive)
    probs = jnp.exp(scores_again - log_total)
    probs_again_low = probs.astype(jnp.bfloat16)
    grad_probs = jnp.einsum(
        "ishd,ithd->ihst", grad_attended, value_rows, preferred_element_type=jnp.float32
    )
    inner_sum = jnp.sum(probs * grad_probs, -1, keepdims=True)
    grad_scores = (probs * (grad_probs - inner_sum)).astype(jnp.bfloat16)
    grad_query = jnp.einsum(
        "ihst,ithd->ishd", grad_scores, key_rows, preferred_element_type=jnp.float32
    ) * HEAD_DIM ** (-0.5)
    grad_key = jnp.einsum(
        "ihst,ishd->ithd", grad_scores, query_rows, preferred_element_type=jnp.float32
    ) * HEAD_DIM ** (-0.5)
    grad_value = jnp.einsum(
        "ihst,ishd->ithd", probs_again_low, grad_attended, preferred_element_type=jnp.float32
    )
    stacked = jnp.stack([grad_query, grad_key, grad_value], 2).astype(jnp.bfloat16)
    stacked = stacked.reshape(attn_images, length_all, 3, 1, group_width)
    grad_qkv = lax.all_to_all(stacked, "head", split_axis=0, concat_axis=3, tiled=True).reshape(
        row_count, 3 * features
    )
    grad_qkv_weight = across(normed_low, grad_qkv)
    qkv_sums = jnp.sum(grad_qkv.astype(jnp.float32), 0)
    grad_normed = against(grad_qkv, w_qkv).reshape(images, length_all, features)
    grad_in_norm, gain_first, shift_first = pull_first(grad_normed)
    input_grad = grad_middle.reshape(images, length_all, features) + grad_in_norm
    vector_rows = jnp.stack(
        [
            gain_first,
            shift_first,
            qkv_sums[:features],
            qkv_sums[2 * features :],
            bias_proj,
            gain_second,
            shift_second,
            bias_fc2,
        ]
    )
    grad_vec = jnp.concatenate([vector_rows, bias_fc1.reshape(-1, features)], 0)
    gradients = (grad_qkv_weight, grad_proj, grad_fc1, grad_fc2, grad_vec)
    summed = (
        lax.psum(gradients[0].astype(jnp.bfloat16), "head").astype(jnp.float32),
        lax.psum(gradients[1].astype(jnp.bfloat16), "head").astype(jnp.float32),
        lax.psum(gradients[2].astype(jnp.bfloat16), "head").astype(jnp.float32),
        lax.psum(gradients[3].astype(jnp.bfloat16), "head").astype(jnp.float32),
        lax.psum(gradients[4].astype(jnp.bfloat16), "head").astype(jnp.float32),
    )
    shares = (
        lax.psum_scatter(summed[0], "dp", scatter_dimension=0, tiled=True),
        lax.psum_scatter(summed[1], "dp", scatter_dimension=0, tiled=True),
        lax.psum_scatter(summed[2], "dp", scatter_dimension=0, tiled=True),
        lax.psum_scatter(summed[3], "dp", scatter_dimension=0, tiled=True),
        lax.psum_scatter(summed[4], "dp", scatter_dimension=1, tiled=True),
    )
    qkv_state = adamw(qkv_master, qkv_first, qkv_second, shares[0], step_rates[0], decays[0])
    proj_state = adamw(proj_master, proj_first, proj_second, shares[1], step_rates[1], decays[1])
    fc1_state = adamw(fc1_master, fc1_first, fc1_second, shares[2], step_rates[2], decays[2])
    fc2_state = adamw(fc2_master, fc2_first, fc2_second, shares[3], step_rates[3], decays[3])
    vec_state = adamw(vec_master, vec_first, vec_second, shares[4], step_rates[4], decays[4])
    return (
        layer_out,
        input_grad,
        qkv_state[0],
        qkv_state[1],
        qkv_state[2],
        proj_state[0],
        proj_state[1],
        proj_state[2],
        fc1_state[0],
        fc1_state[1],
        fc1_state[2],
        fc2_state[0],
        fc2_state[1],
        fc2_state[2],
        vec_state[0],
        vec_state[1],
        vec_state[2],
    )


def solution(mesh):
    return jax.shard_map(
        on_device,
        mesh=mesh,
        in_specs=(
            P(("dp", "head"), None, None),
            P(("dp", "head"), None, None),
            P(("dp", "head"), None),
            P(("dp", "head")),
            P("dp", None),
            P("dp", None),
            P("dp", None),
            P("dp", None),
            P(None, "dp"),
            P("dp", None),
            P("dp", None),
            P("dp", None),
            P("dp", None),
            P(None, "dp"),
            P("dp", None),
            P("dp", None),
            P("dp", None),
            P("dp", None),
            P(None, "dp"),
        ),
        out_specs=(
            P(("dp", "head"), None, None),
            P(("dp", "head"), None, None),
            P("dp", None),
            P("dp", None),
            P("dp", None),
            P("dp", None),
            P("dp", None),
            P("dp", None),
            P("dp", None),
            P("dp", None),
            P("dp", None),
            P("dp", None),
            P("dp", None),
            P("dp", None),
            P(None, "dp"),
            P(None, "dp"),
            P(None, "dp"),
        ),
        check_vma=False,
    )
```

profile of v0, /device:TPU:0, one launch (start us, length us, event | category | flops | bytes accessed | tf_op | source)
XLA Modules:
  0.0 1007.1 jit_solution(7411989517168718073)
XLA Ops:
  8.0 42.7 %all-gather = bf16[16,24,12]{1,2,0:T(8,128)(2,1)S(1)} all-gather(bf16[1,24,12]{1,2,0:T(8,128)(2,1)S(1)} %convert_bitcast_fusion), channel_id=1, replica_groups=mesh['dp'=16,'head'=2] {'dp'}, dimensions={0}, use_global_device_ids=true | all-gather | bytes 9792 | tf_op jit(solution)/shard_map/all_gather | solution.py:80
  54.4 36.9 %psum.42 = f32[96]{0:T(128)S(1)} all-reduce(f32[96]{0:T(128)S(1)} %select_reduce_fusion.1), channel_id=1, replica_groups=mesh['dp'=16,'head'=2] {'dp','head'}, use_global_device_ids=true, to_apply=%region_8.9 | all-reduce | flops 96 | bytes 768 | tf_op jit(solution)/shard_map/psum | solution.py:94
  92.6 44.3 %all_gather.16 = bf16[384,1152]{1,0:T(8,128)(2,1)S(1)} all-gather(bf16[24,1152]{1,0:T(8,128)(2,1)S(1)} %convert_element_type.145), channel_id=1, replica_groups=mesh['dp'=16,'head'=2] {'dp'}, dimensions={0}, use_global_device_ids=true | all-gather | bytes 940032 | tf_op jit(solution)/shard_map/all_gather | solution.py:76
  137.9 4.5 fusion.8
  142.5 12.9 %reshape.248 = bf16[9,198,3,2,192]{4,3,2,1,0:T(2,128)(2,1)} reshape(bf16[1782,1152]{1,0:T(8,128)(2,1)} %fusion.8) | data formatting | bytes 8211456 | tf_op jit(solution)/shard_map/reshape | solution.py:103
  155.3 17.4 %copy.110 = bf16[9,198,3,2,192]{1,4,2,0,3:T(8,128)(2,1)} copy(bf16[9,198,3,2,192]{4,3,2,1,0:T(2,128)(2,1)} %reshape.248) | data formatting | bytes 8211456 | tf_op jit(solution)/shard_map/reshape | solution.py:103
  172.8 6.1 all-to-all-start
  180.4 3.8 all-to-all-done
  184.2 3.8 all-to-all-start.1
  187.9 5.4 copy.111
  193.5 4.4 fusion.13
  198.0 3.2 fusion.6
  202.2 5.5 fusion.31
  207.7 3.8 all-to-all-start.2
  212.4 1.8 all-to-all-done.2
  215.3 5.6 copy.114
  222.0 37.8 %all_gather.17 = bf16[384,384]{1,0:T(8,128)(2,1)S(1)} all-gather(bf16[24,384]{1,0:T(8,128)(2,1)S(1)} %convert_element_type.151), channel_id=1, replica_groups=mesh['dp'=16,'head'=2] {'dp'}, dimensions={0}, use_global_device_ids=true | all-gather | bytes 313344 | tf_op jit(solution)/shard_map/all_gather | solution.py:77
  259.9 2.7 convolution_add_fusion.1
  262.6 3.5 reshape.252
  266.1 2.6 fusion.61
  271.0 3.0 convert_element_type.153
  274.0 3.4 fusion.51
  277.4 3.0 convert_element_type.161
  280.4 28.8 %multiply_convert_fusion.1 = (bf16[1782,1536]{1,0:T(8,128)(2,1)}, f32[1782,1536]{1,0:T(8,128)}, f32[1782,1536]{1,0:T(8,128)}) fusion(f32[1536]{0:T(1024)S(1)} %add.213, bf16[1782,384]{1,0:T(8,128)(2,1)} %convert_element_type.153, bf16[384,1536]{1,0:T(8,128)(2,1)} %all-gather.4.cloned.1.call-done), kind=kOutput, calls=%fused_computation.9 | convolution fusion | flops 2282784768 | bytes 29925888 | tf_op jit(solution)/shard_map/dot_general | solution.py:140
  309.1 13.2 %fusion.63 = (bf16[1536]{0:T(1024)(128)(2,1)S(1)}, bf16[1782,1536]{1,0:T(8,128)(2,1)S(1)}) fusion(f32[1782,1536]{1,0:T(8,128)} %get-tuple-element.59, bf16[1782,384]{1,0:T(8,128)(2,1)} %convert_element_type.161, bf16[1536,384]{1,0:T(8,128)(2,1)} %all-gather.6.cloned.1.call-done, f32[1782,1536]{1,0:T(8,128)} %get-tuple-element.64, f32[1536]{0:T(1024)S(1)} %add.213), kind=kOutput, calls=%fused_computation.139 | convolution fusion | flops 2145925632 | bytes 29928960 | tf_op jit(solution)/shard_map/dot_general | solution.py:34
  322.3 4.7 fusion.62
  327.0 3.4 reshape.255
  330.4 3.0 multiply_reduce_fusion.1
  334.9 2.0 fusion.53
  336.9 3.0 convert_element_type.164
  339.9 3.5 convolution_convert_fusion.3
  343.4 5.4 reshape.256
  348.8 6.6 copy.115
  355.4 6.6 all_to_all.69
  362.0 10.8 %multiply_reduce_fusion = (f32[18,3,198]{2,1,0:T(4,128)S(1)}, f32[18,3,198,198]{2,3,1,0:T(8,128)}) fusion(f32[18,3,198]{2,1,0:T(4,128)S(1)} %log_add_fusion, f32[18,3,198,198]{2,3,1,0:T(8,128)} %copy-done, pred[18,198]{1,0:T(8,128)(4,1)S(1)} %gt.23, bf16[18,198,3,64]{1,3,2,0:T(8,128)(2,1)S(1)} %bitcast.120, bf16[18,198,3,3,64]{1,4,3,0,2:T(8,128)(2,1)} %bitcast.117), kind=kOutput, calls=%fused_computation.2 | convolution fusion | flops 281552448 | bytes 22754412 | tf_op jit(solution)/shard_map/ishd,ithd->ihst/dot_general | solution.py:179
  372.8 6.6 multiply_convert_fusion
  379.4 2.7 multiply_convert_fusion.3
  382.0 4.6 multiply_convert_fusion.2
  386.6 4.3 fusion.28
  390.9 6.5 convolution_convert_fusion.1
  400.1 9.5 all_to_all.70
  409.7 17.6 %copy.122 = bf16[9,198,3,2,1,192]{5,3,2,1,0,4:T(2,128)(2,1)} copy(bf16[9,198,3,2,1,192]{1,5,4,2,0,3:T(8,128)(2,1)} %bitcast.113) | data formatting | bytes 8211456 | tf_op jit(solution)/shard_map/all_to_all | solution.py:195
  427.3 11.9 %reshape.258 = bf16[1782,1152]{1,0:T(8,128)(2,1)} reshape(bf16[9,198,3,2,1,192]{5,3,2,1,0,4:T(2,128)(2,1)} %copy.122) | data formatting | bytes 8211456 | tf_op jit(solution)/shard_map/reshape | solution.py:195
  439.2 5.6 convolution_convert_fusion.2
  444.8 6.7 convolution_convert_fusion
  451.6 22.1 %all-reduce.6.cloned.1.call-done = (bf16[384,1152]{1,0:T(8,128)(2,1)}, bf16[384,384]{1,0:T(8,128)(2,1)}, bf16[384,1536]{1,0:T(8,128)(2,1)}, bf16[1536,384]{1,0:T(8,128)(2,1)}) async-done(((bf16[384,1152]{1,0:T(8,128)(2,1)}, bf16[384,384]{1,0:T(8,128)(2,1)}, bf16[384,1536]{1,0:T(8,128)(2,1)}, bf16[1536,384]{1,0:T(8,128)(2,1)}), (bf16[384,1152]{1,0:T(8,128)(2,1)}, bf16[384,384]{1,0:T(8,128)(2,1)}, ...) | async-done | bytes 3538960 | tf_op jit(solution)/shard_map/psum | solution.py:218
  473.7 1.8 convert_element_type.171
  475.6 2.5 convert_element_type.169
  478.2 2.8 convert_element_type.175
  481.1 3.1 convert_element_type.173
  484.2 1.8 reshape.253
  487.3 9.8 dot_general.70
  497.2 5.2 fusion.49
  505.6 3.6 reduce.5
  509.5 7.6 fusion.21
  517.1 3.1 reshape.254
  520.3 3.4 psum.47
  523.6 77.2 %all-reduce.2 = f32[12,384]{1,0:T(8,128)S(1)} all-reduce(bf16[12,384]{1,0:T(8,128)(2,1)S(1)} %psum.47), channel_id=6, replica_groups=mesh['dp'=16,'head'=2] {'dp'}, use_global_device_ids=true, to_apply=%region_32.33.clone | all-reduce | flops 4608 | bytes 27648
  601.6 5.8 add_add_fusion.2
  608.9 123.8 %reduce-scatter.14.cloned.1.call-done = f32[24,1152]{1,0:T(8,128)} async-done(((f32[384,1152]{1,0:T(8,128)}), f32[24,1152]{1,0:T(8,128)}) %reduce-scatter.14.cloned.1.call-update) | async-done | bytes 110608
  734.5 130.4 %reduce-scatter.12.cloned.1.call-done = f32[96,384]{1,0:T(8,128)} async-done(((f32[1536,384]{1,0:T(8,128)}), f32[96,384]{1,0:T(8,128)}) %reduce-scatter.12.cloned.1.call-update) | async-done | bytes 147472 | tf_op jit(solution)/shard_map/reduce_scatter | solution.py:228
  864.9 1.8 multiply_subtract_fusion
  866.7 131.5 %reduce-scatter.10.cloned.1.call-done = f32[24,1536]{1,0:T(8,128)} async-done(((f32[384,1536]{1,0:T(8,128)}), f32[24,1536]{1,0:T(8,128)}) %reduce-scatter.10.cloned.1.call-update) | async-done | bytes 147472 | tf_op jit(solution)/shard_map/reduce_scatter | solution.py:227
  998.2 1.9 multiply_subtract_fusion.1
  (178 shorter events, 27.2 us)
Async XLA Ops:
  7.2 46.0 %copy-start.1 = (bf16[9,198,384]{2,1,0:T(8,128)(2,1)S(1)}, bf16[9,198,384]{2,1,0:T(8,128)(2,1)}, u32[]{:S(2)}) copy-start(bf16[9,198,384]{2,1,0:T(8,128)(2,1)} %param.19) | copy-start | bytes 4105732
  7.2 47.0 %copy-start.32 = (s32[9,198]{1,0:T(8,128)S(1)}, s32[9,198]{1,0:T(8,128)}, u32[]{:S(2)}) copy-start(s32[9,198]{1,0:T(8,128)} %param.21) | copy-start | bytes 21388
  7.2 47.1 %copy-start.45 = (s32[9]{0:T(128)S(1)}, s32[9]{0:T(128)}, u32[]{:S(2)}) copy-start(s32[9]{0:T(128)} %param.22) | copy-start | bytes 112
  51.5 40.8 %copy-start.37 = (f32[384]{0:T(512)}, f32[384]{0:T(512)S(1)}, u32[]{:S(2)}) copy-start(f32[384]{0:T(512)S(1)} %get-tuple-element.30) | copy-start | bytes 4612
  53.2 39.4 %copy-start.24 = (f32[9,198]{1,0:T(8,128)}, f32[9,198]{1,0:T(8,128)S(1)}, u32[]{:S(2)}) copy-start(f32[9,198]{1,0:T(8,128)S(1)} %broadcast_multiply_fusion.1) | copy-start | bytes 21388
  54.2 38.0 %copy-start.28 = (f32[9,198]{1,0:T(8,128)}, f32[9,198]{1,0:T(8,128)S(1)}, u32[]{:S(2)}) copy-start(f32[9,198]{1,0:T(8,128)S(1)} %fusion.25) | copy-start | bytes 21388
  91.6 1.0 copy-start.26
  91.6 1.0 copy-start.22
  92.6 49.9 %copy-start.14 = (bf16[1782,384]{1,0:T(8,128)(2,1)}, bf16[1782,384]{1,0:T(8,128)(2,1)S(1)}, u32[]{:S(2)}) copy-start(bf16[1782,384]{1,0:T(8,128)(2,1)S(1)} %convert_element_type.144) | copy-start | bytes 4105732
  137.0 1.0 copy-start.16
  172.8 6.2 copy-start.20
  172.8 11.4 %all-to-all-start = ((bf16[9,198,3,2,192]{1,4,2,0,3:T(8,128)(2,1)}), bf16[9,198,3,2,192]{1,4,2,0,3:T(8,128)(2,1)}, u32[]{:S(2)}, u32[]{:S(2)}) async-start(bf16[9,198,3,2,192]{1,4,2,0,3:T(8,128)(2,1)} %copy.110), calls=%async_computation | async-start | bytes 10616832 | tf_op jit(solution)/shard_map/all_to_all | solution.py:108
  178.9 101.4 %all-gather.4.cloned.1.call-start = ((), (), s32[]{:S(2)}) async-start(), calls=%async_computation.9 | async-start | bytes 1253376 | tf_op jit(solution)/shard_map/all_gather | solution.py:78
  184.2 9.2 all-to-all-start.1
  198.0 4.2 copy-start
  207.7 3.9 copy-start.18
  207.7 6.5 all-to-all-start.2
  211.5 97.6 %all-gather.6.cloned.1.call-start = ((), (), s32[]{:S(2)}) async-start(), calls=%async_computation.10 | async-start | bytes 1253376 | tf_op jit(solution)/shard_map/all_gather | solution.py:79
  212.3 261.4 %all-reduce.6.cloned.1.call-start = ((), (), s32[]{:S(2)}) async-start(), calls=%async_computation.15 | async-start | bytes 7077888 | tf_op jit(solution)/shard_map/psum | solution.py:218
  214.1 1.2 copy-start.11
  215.3 6.7 copy-start.30
  222.0 40.6 %copy-start.7 = (bf16[1782,384]{1,0:T(8,128)(2,1)}, bf16[1782,384]{1,0:T(8,128)(2,1)S(1)}, u32[]{:S(2)}) copy-start(bf16[1782,384]{1,0:T(8,128)(2,1)S(1)} %reshape.251) | copy-start | bytes 4105732
  309.1 13.2 %copy-start.44 = (bf16[384,1536]{1,0:T(8,128)(2,1)S(1)}, bf16[384,1536]{1,0:T(8,128)(2,1)}, u32[]{:S(2)}) copy-start(bf16[384,1536]{1,0:T(8,128)(2,1)} %all-gather.4.cloned.1.call-done) | copy-start | bytes 3538948
  322.3 4.7 copy-start.47
  330.4 3.0 copy-start.3
  333.4 1.5 copy-start.5
  334.9 2.0 copy-start.4
  362.0 10.8 %slice-start = ((s8[11059200]{0:T(1024)(128)(4,1)}), s8[4194304]{0:T(1024)(128)(4,1)S(1)}, s32[]{:S(2)}) async-start(s8[11059200]{0:T(1024)(128)(4,1)} %bitcast.111), calls=%async_computation.16 | async-start | bytes 8388608
  362.0 10.8 %slice-start.1 = ((s8[11059200]{0:T(1024)(128)(4,1)}), s8[4194304]{0:T(1024)(128)(4,1)S(1)}, s32[]{:S(2)}) async-start(s8[11059200]{0:T(1024)(128)(4,1)} %bitcast.111), calls=%async_computation.17 | async-start | bytes 8388608
  362.0 10.8 %slice-start.2 = ((s8[11059200]{0:T(1024)(128)(4,1)}), s8[2670592]{0:T(1024)(128)(4,1)S(1)}, s32[]{:S(2)}) async-start(s8[11059200]{0:T(1024)(128)(4,1)} %bitcast.111), calls=%async_computation.18 | async-start | bytes 5341184
  390.9 6.5 copy-start.8
  390.9 6.5 copy-start.9
  390.9 8.1 copy-start.13
  397.4 1.6 copy-start.12
  439.2 5.6 copy-start.15
  451.5 155.9 %reduce-scatter.16.cloned.1.call-start = ((), (), s32[]{:S(2)}) async-start(), calls=%async_computation.14 | async-start | bytes 626688
  475.6 257.1 %reduce-scatter.14.cloned.1.call-start = ((), (), s32[]{:S(2)}) async-start(), calls=%async_computation.13 | async-start | bytes 1880064
  478.2 386.7 %reduce-scatter.12.cloned.1.call-start = ((), (), s32[]{:S(2)}) async-start(), calls=%async_computation.12 | async-start | bytes 2506752 | tf_op jit(solution)/shard_map/reduce_scatter | solution.py:228
  481.1 517.1 %reduce-scatter.10.cloned.1.call-start = ((), (), s32[]{:S(2)}) async-start(), calls=%async_computation.11 | async-start | bytes 2506752 | tf_op jit(solution)/shard_map/reduce_scatter | solution.py:227
  484.2 1.8 copy-start.41
  484.2 1.8 copy-start.46
  487.3 9.8 copy-start.2
  487.3 9.8 copy-start.17
  487.3 9.8 copy-start.25
  487.3 9.8 copy-start.38
  497.1 5.2 copy-start.29
  497.1 6.8 copy-start.27
  502.4 1.6 copy-start.10
  505.6 3.9 copy-start.42
  505.6 3.9 copy-start.43
  517.1 83.7 %copy-start.36 = (f32[12,24]{1,0:T(8,128)S(1)}, f32[12,24]{1,0:T(8,128)}, u32[]{:S(2)}) copy-start(f32[12,24]{1,0:T(8,128)} %param.27) | copy-start | bytes 3460
  517.1 83.7 %copy-start.39 = (f32[12,24]{1,0:T(8,128)S(1)}, f32[12,24]{1,0:T(8,128)}, u32[]{:S(2)}) copy-start(f32[12,24]{1,0:T(8,128)} %param.37) | copy-start | bytes 3460
  517.1 83.7 %copy-start.40 = (f32[12,24]{1,0:T(8,128)S(1)}, f32[12,24]{1,0:T(8,128)}, u32[]{:S(2)}) copy-start(f32[12,24]{1,0:T(8,128)} %param.32) | copy-start | bytes 3460
  517.1 84.5 %copy-start.6 = (bf16[9,198,384]{2,1,0:T(8,128)(2,1)S(1)}, bf16[9,198,384]{2,1,0:T(8,128)(2,1)}, u32[]{:S(2)}) copy-start(bf16[9,198,384]{2,1,0:T(8,128)(2,1)} %param.20) | copy-start | bytes 4105732
  601.6 5.8 copy-start.31
  601.6 5.8 copy-start.34
  601.6 5.8 copy-start.35
  601.6 131.1 %copy-start.23 = (f32[24,1152]{1,0:T(8,128)S(1)}, f32[24,1152]{1,0:T(8,128)}, u32[]{:S(2)}) copy-start(f32[24,1152]{1,0:T(8,128)} %param.23) | copy-start | bytes 331780
  601.6 263.3 %copy-start.19 = (f32[96,384]{1,0:T(8,128)S(1)}, f32[96,384]{1,0:T(8,128)}, u32[]{:S(2)}) copy-start(f32[96,384]{1,0:T(8,128)} %param.26) | copy-start | bytes 442372
  601.6 263.3 %copy-start.33 = (f32[96,384]{1,0:T(8,128)S(1)}, f32[96,384]{1,0:T(8,128)}, u32[]{:S(2)}) copy-start(f32[96,384]{1,0:T(8,128)} %param.36) | copy-start | bytes 442372
  601.6 396.6 %copy-start.21 = (f32[24,1536]{1,0:T(8,128)S(1)}, f32[24,1536]{1,0:T(8,128)}, u32[]{:S(2)}) copy-start(f32[24,1536]{1,0:T(8,128)} %param.25) | copy-start | bytes 442372
Sparse Core Ops, SparseCore 0:
  183.1 53.1 all-gather.3
  239.7 55.1 all-gather.5
  451.6 22.0 all-reduce.5
  479.0 123.3 reduce-scatter.15
  607.0 125.5 reduce-scatter.13
  737.5 127.3 reduce-scatter.11
  870.6 127.5 reduce-scatter.9
where the time goes:
time: 1020 us; the launch traced here: 1010 us
  waiting for transfers between devices  414 us (41%)
  blocking collectives  258 us (25%)
  matrix products  123 us (12%)
  local copies, waits for them, and re-layouts  122 us (12%)
  other arithmetic  60.4 us (6%)
  between operations  15.7 us (2%)
  starting transfers between devices  14 us (1%)
    reduce_scatter x1, waiting for transfers between devices, on_device(): lax.psum_scatter(summed[2], 'dp', scatter_dimension=0, tiled=True)  131 us
    reduce_scatter x1, waiting for transfers between devices, on_device(): lax.psum_scatter(summed[3], 'dp', scatter_dimension=0, tiled=True)  130 us
    unnamed x9, waiting for transfers between devices  124 us
    unnamed x1, blocking collectives  77.2 us
    all_gather x1, blocking collectives, on_device(): lax.all_gather(qkv_master.astype(jnp.bfloat16), 'dp', axis=0, tiled=True)  44.3 us
    all_gather x1, blocking collectives, on_device(): lax.all_gather(vec_master.astype(jnp.bfloat16), 'dp', axis=1, tiled=True)  42.7 us
    all_gather x1, blocking collectives, on_device(): lax.all_gather(proj_master.astype(jnp.bfloat16), 'dp', axis=0, tiled=True)  37.8 us
    psum x1, blocking collectives, on_device(): totals = lax.psum(jnp.sum(onehot * kept_rows[:, None], 0), ('dp', 'head'))  36.9 us
  transfers between devices with their start and end apart: 10, of which 6 were waited for; matrix products, arithmetic and copies ran while one was open for 13% of the time, Pallas kernels for 0%

commit v1 on v0

v1 whole, which is shorter than its diff:
```python
import functools

import jax
import jax.numpy as jnp
from jax import lax
from jax.experimental import pallas as pl
from jax.experimental.pallas import tpu as pltpu
from jax.sharding import PartitionSpec as P

HEADS = 6
HEAD_DIM = 64
STEP = 10
PAIRS = HEADS // 2
SCALE = HEAD_DIM ** (-0.5)

norm_eps = 1e-06
step_rates = (0.1, 0.4, 0.1, 0.05, 0.5)
decays = (0.05, 0.05, 0.05, 0.05, 0.0)

F32 = jnp.float32
BF16 = jnp.bfloat16


def dot(left, right):
    return lax.dot_general(left, right, (((1,), (0,)), ((), ())), preferred_element_type=F32)


def across(left, right):
    return lax.dot_general(left, right, (((0,), (0,)), ((), ())), preferred_element_type=F32)


def against(left, right):
    return lax.dot_general(left, right, (((1,), (1,)), ((), ())), preferred_element_type=F32)


def normalise(values):
    average = jnp.mean(values, -1, keepdims=True)
    centred = values - average
    variance = jnp.mean(centred * centred, -1, keepdims=True)
    inverse = lax.rsqrt(variance + norm_eps)
    return centred * inverse, inverse


def norm_back(grad, unit, inverse, gain_row):
    scaled = grad * gain_row
    first = jnp.mean(scaled, -1, keepdims=True)
    second = jnp.mean(scaled * unit, -1, keepdims=True)
    return inverse * (scaled - first - unit * second)


def fold(values):
    rows, cols = values.shape
    return jnp.sum(values.reshape(rows // 8, 8, cols), 0)


ERF_A = (0.254829592, -0.284496736, 1.421413741, -1.453152027, 1.061405429)
ERF_C = 0.3275911 * 0.7071067811865476
LOG2E_HALF = 0.7213475204444817
INV_SQRT_2PI = 0.3989422804014327


def gelu_parts(x):
    bell = jnp.exp2(x * x * (-LOG2E_HALF))
    t = 1.0 / (1.0 + ERF_C * jnp.abs(x))
    a1, a2, a3, a4, a5 = (0.5 * a for a in ERF_A)
    tail = ((((a5 * t + a4) * t + a3) * t + a2) * t + a1) * t * bell
    cdf = jnp.where(x >= 0, 1.0 - tail, tail)
    return x * cdf, cdf + x * (bell * INV_SQRT_2PI)


def layer_kernel(
    tok_ref, cot_ref, keep_ref, tw_ref, wq_ref, wp_ref, w1_ref, w2_ref, vec_ref,
    out_ref, gin_ref, gq_ref, gp_ref, g1_ref, g2_ref, gvec_ref,
    xs, normed, qkv, probs, att, middle, nmid, act, gel, gol, gms, gml, twc, sums,
    stages=99,
):
    images, length, feat = tok_ref.shape
    padded = xs.shape[1]
    hidden_units = w1_ref.shape[1] // feat
    lane = lax.broadcasted_iota(jnp.int32, (padded, 128), 1)
    low_half = lane < HEAD_DIM

    def each_image(body):
        lax.fori_loop(0, images, lambda i, c: (body(i), c)[1], 0)

    def row(n):
        return vec_ref[n : n + 1, :]

    def stacked_halves(values):
        zero = jnp.zeros_like(values)
        return jnp.concatenate(
            [jnp.where(low_half, values, zero), jnp.where(low_half, zero, values)], 0
        )

    def merged_halves(values):
        return jnp.where(low_half, values[:padded], values[padded:])

    tail = padded - 16
    xs[:, tail:, :] = jnp.zeros((images, 16, feat), BF16)
    gol[:, tail:, :] = jnp.zeros((images, 16, feat), BF16)
    sums[...] = jnp.zeros_like(sums)

    eye = lax.broadcasted_iota(jnp.int32, (padded, padded), 0) == lax.broadcasted_iota(
        jnp.int32, (padded, padded), 1
    )

    def first_norm(i):
        xs[i, 0:length, :] = tok_ref[i]
        unit, _ = normalise(xs[i].astype(F32))
        normed[i] = (unit * row(0) + row(1)).astype(BF16)
        weight_row = tw_ref[pl.ds(i, 1), :]
        column = jnp.sum(jnp.where(eye, weight_row, 0.0), 1, keepdims=True)
        twc[i] = jnp.broadcast_to(column, (padded, 128))
        wide = jnp.concatenate([twc[i]] * (feat // 128), 1)[:length]
        gol[i, 0:length, :] = (cot_ref[i].astype(F32) * wide).astype(BF16)

    each_image(first_norm)
    if stages <= 1:
        return

    def project(i):
        values = normed[i]
        for h in range(PAIRS):
            part = pl.ds(128 * h, 128)
            bias = jnp.concatenate(
                [vec_ref[2:3, part], jnp.zeros((1, 128), F32), vec_ref[3:4, part]], 1
            )
            qkv[h, i] = (dot(values, wq_ref[h]) + bias).astype(BF16)

    each_image(project)
    if stages <= 2:
        return

    def attend(i):
        alive = keep_ref[pl.ds(i, 1), :] > 0
        for h in range(PAIRS):
            query = stacked_halves(qkv[h, i, :, 0:128] * BF16(SCALE))
            scores = against(query, qkv[h, i, :, 128:256])
            scores = jnp.where(alive, scores, -1e9)
            top = jnp.max(scores, -1, keepdims=True)
            raised = jnp.exp(scores - top)
            share = raised * (1.0 / jnp.sum(raised, -1, keepdims=True))
            share = share.astype(BF16)
            probs[h, i] = share
            att[i, :, 128 * h : 128 * h + 128] = merged_halves(
                dot(share, qkv[h, i, :, 256:384])
            ).astype(BF16)

    each_image(attend)
    if stages <= 3:
        return

    def second_norm(i):
        mid = xs[i].astype(F32) + (dot(att[i], wp_ref[...]) + row(4))
        middle[i] = mid
        unit, _ = normalise(mid)
        nmid[i] = (unit * row(5) + row(6)).astype(BF16)

    each_image(second_norm)
    if stages <= 4:
        return

    def expand(i):
        values = nmid[i]
        for j in range(hidden_units):
            cols = slice(feat * j, feat * j + feat)
            pre = dot(values, w1_ref[:, cols]) + row(8 + j)
            active, slope = gelu_parts(pre)
            act[i, :, cols] = active.astype(BF16)
            gel[i, :, cols] = slope.astype(BF16)

    each_image(expand)
    if stages <= 5:
        return

    def contract(i):
        total = middle[i] + (dot(act[i], w2_ref[...]) + row(7))
        out_ref[i] = total[:length].astype(BF16)

    each_image(contract)
    if stages <= 6:
        return

    def hidden_back(i):
        grad = gol[i]
        sums[7] += fold(grad.astype(F32))
        for j in range(hidden_units):
            cols = slice(feat * j, feat * j + feat)
            back = against(grad, w2_ref[cols, :]) * gel[i, :, cols].astype(F32)
            back = back.astype(BF16)
            gel[i, :, cols] = back
            sums[8 + j] += fold(back.astype(F32))

    each_image(hidden_back)
    if stages <= 7:
        return

    g2_ref[...] = jnp.zeros_like(g2_ref)

    def fc2_grad(i):
        for j in range(hidden_units):
            cols = slice(feat * j, feat * j + feat)
            g2_ref[cols, :] += across(act[i, :, cols], gol[i])

    each_image(fc2_grad)
    if stages <= 8:
        return

    def middle_back(i):
        unit, inverse = normalise(middle[i])
        grad = against(gel[i], w1_ref[...])
        sums[5] += fold(grad * unit)
        sums[6] += fold(grad)
        back = norm_back(grad, unit, inverse, row(5))
        wide = jnp.concatenate([twc[i]] * (feat // 128), 1)[:length]
        gms[i] = back
        gms[i, 0:length, :] += cot_ref[i].astype(F32) * wide
        low = gms[i].astype(BF16)
        gml[i] = low
        sums[4] += fold(low.astype(F32))

    each_image(middle_back)
    if stages <= 9:
        return

    g1_ref[...] = jnp.zeros_like(g1_ref)
    gp_ref[...] = jnp.zeros_like(gp_ref)

    def fc1_grad(i):
        for j in range(hidden_units):
            cols = slice(feat * j, feat * j + feat)
            g1_ref[:, cols] += across(nmid[i], gel[i, :, cols])
        gp_ref[...] += across(att[i], gml[i])

    each_image(fc1_grad)
    if stages <= 10:
        return

    def attend_back(i):
        grad_att = against(gml[i], wp_ref[...]).astype(BF16)
        for h in range(PAIRS):
            grad = stacked_halves(grad_att[:, 128 * h : 128 * h + 128])
            key = qkv[h, i, :, 128:256]
            query = stacked_halves(qkv[h, i, :, 0:128] * BF16(SCALE))
            share_low = probs[h, i]
            share = share_low.astype(F32)
            grad_share = against(grad, qkv[h, i, :, 256:384])
            inner = jnp.sum(share * grad_share, -1, keepdims=True)
            grad_score = (share * (grad_share - inner)).astype(BF16)
            grad_query = (merged_halves(dot(grad_score, key)) * SCALE).astype(BF16)
            grad_key = across(grad_score, query).astype(BF16)
            grad_value = across(share_low, grad).astype(BF16)
            qkv[h, i, :, 0:128] = grad_query
            qkv[h, i, :, 128:256] = grad_key
            qkv[h, i, :, 256:384] = grad_value
            part = slice(128 * h, 128 * h + 128)
            sums[2, :, part] += fold(grad_query.astype(F32))
            sums[3, :, part] += fold(grad_value.astype(F32))

    each_image(attend_back)
    if stages <= 11:
        return

    gq_ref[...] = jnp.zeros_like(gq_ref)

    def qkv_grad(i):
        for h in range(PAIRS):
            gq_ref[h] += across(normed[i], qkv[h, i])

    each_image(qkv_grad)
    if stages <= 12:
        return

    def input_back(i):
        unit, inverse = normalise(xs[i].astype(F32))
        grad = against(qkv[0, i], wq_ref[0])
        for h in range(1, PAIRS):
            grad = grad + against(qkv[h, i], wq_ref[h])
        sums[0] += fold(grad * unit)
        sums[1] += fold(grad)
        total = gms[i] + norm_back(grad, unit, inverse, row(0))
        gin_ref[i] = total[:length]

    each_image(input_back)
    for n in range(12):
        gvec_ref[n : n + 1, :] = jnp.sum(sums[n], 0, keepdims=True)


def run_layer(tokens, cotangent, keep, weight, wq, wp, w1, w2, vec, stages=99):
    images, length, feat = tokens.shape
    padded = -(-length // 16) * 16
    hidden = w1.shape[1]
    vmem = pl.BlockSpec(memory_space=pltpu.VMEM)
    shape = jax.ShapeDtypeStruct
    keep = jnp.pad(keep.astype(F32), ((0, 0), (0, padded - length)))
    weight = jnp.pad(weight, ((0, 0), (0, padded - length)))
    return pl.pallas_call(
        functools.partial(layer_kernel, stages=stages),
        out_shape=(
            shape((images, length, feat), BF16),
            shape((images, length, feat), F32),
            shape(wq.shape, F32),
            shape(wp.shape, F32),
            shape(w1.shape, F32),
            shape(w2.shape, F32),
            shape(vec.shape, F32),
        ),
        in_specs=[vmem] * 9,
        out_specs=[vmem] * 7,
        scratch_shapes=[
            pltpu.VMEM((images, padded, feat), BF16),
            pltpu.VMEM((images, padded, feat), BF16),
            pltpu.VMEM((PAIRS, images, padded, feat), BF16),
            pltpu.VMEM((PAIRS, images, 2 * padded, padded), BF16),
            pltpu.VMEM((images, padded, feat), BF16),
            pltpu.VMEM((images, padded, feat), F32),
            pltpu.VMEM((images, padded, feat), BF16),
            pltpu.VMEM((images, padded, hidden), BF16),
            pltpu.VMEM((images, padded, hidden), BF16),
            pltpu.VMEM((images, padded, feat), BF16),
            pltpu.VMEM((images, padded, feat), F32),
            pltpu.VMEM((images, padded, feat), BF16),
            pltpu.VMEM((images, padded, 128), F32),
            pltpu.VMEM((12, 8, feat), F32),
        ],
        compiler_params=pltpu.CompilerParams(vmem_limit_bytes=64 * 1024 * 1024),
        name="layer",
    )(tokens, cotangent, keep, weight, wq, wp, w1, w2, vec)


def adamw(master, first, second, gradient, step_rate, weight_decay):
    first_new = 0.9 * first + 0.1 * gradient
    second_new = 0.999 * second + 0.001 * gradient * gradient
    step_size = first_new / (1.0 - 0.9**STEP) / (jnp.sqrt(second_new / (1.0 - 0.999**STEP)) + 1e-08)
    return (first_new, second_new, master - step_rate * (step_size + weight_decay * master))


def by_pair(weight):
    rows, cols = weight.shape
    return weight.reshape(rows, 3, PAIRS, cols // (3 * PAIRS)).transpose(2, 0, 1, 3).reshape(
        PAIRS, rows, cols // PAIRS
    )


def from_pairs(grad):
    pairs, rows, cols = grad.shape
    return grad.reshape(pairs, rows, 3, cols // 3).transpose(1, 2, 0, 3).reshape(rows, pairs * cols)


def on_device(
    tokens, cotangent, keep_mask, source,
    qkv_master, proj_master, fc1_master, fc2_master, vec_master,
    qkv_first, proj_first, fc1_first, fc2_first, vec_first,
    qkv_second, proj_second, fc1_second, fc2_second, vec_second,
):
    gather = functools.partial(lax.all_gather, axis_name="dp", tiled=True)
    w_qkv = gather(qkv_master.astype(BF16), axis=0)
    w_proj = gather(proj_master.astype(BF16), axis=0)
    w_fc1 = gather(fc1_master.astype(BF16), axis=0)
    w_fc2 = gather(fc2_master.astype(BF16), axis=0)
    vectors = gather(vec_master.astype(BF16), axis=1).astype(F32)
    images, length, feat = tokens.shape
    live_mask = keep_mask.astype(F32)
    kept_rows = jnp.sum(live_mask, 1)
    total_sources = images * lax.axis_size("head") * lax.axis_size("dp") // 3
    onehot = (source[:, None] == jnp.arange(total_sources, dtype=jnp.int32)[None, :]).astype(F32)
    totals = lax.psum(jnp.sum(onehot * kept_rows[:, None], 0), ("dp", "head"))
    image_total = jnp.sum(onehot * totals[None, :], 1)
    token_weight = live_mask * (length / image_total)[:, None]
    layer_out, input_grad, gq, gp, g1, g2, gvec = run_layer(
        tokens, cotangent, live_mask, token_weight, by_pair(w_qkv), w_proj, w_fc1, w_fc2, vectors
    )
    gradients = (from_pairs(gq), gp, g1, g2, gvec)
    dims = (0, 0, 0, 0, 1)
    shares = [
        lax.psum_scatter(
            lax.psum(g.astype(BF16), "head").astype(F32), "dp", scatter_dimension=d, tiled=True
        )
        for g, d in zip(gradients, dims)
    ]
    masters = (qkv_master, proj_master, fc1_master, fc2_master, vec_master)
    firsts = (qkv_first, proj_first, fc1_first, fc2_first, vec_first)
    seconds = (qkv_second, proj_second, fc1_second, fc2_second, vec_second)
    states = []
    for parts in zip(masters, firsts, seconds, shares, step_rates, decays):
        states.extend(adamw(*parts))
    return (layer_out, input_grad, *states)


def solution(mesh):
    split = P(("dp", "head"), None, None)
    rows, cols = P("dp", None), P(None, "dp")
    weights = (rows, rows, rows, rows, cols)
    return jax.shard_map(
        on_device,
        mesh=mesh,
        in_specs=(split, split, P(("dp", "head"), None), P(("dp", "head"))) + weights * 3,
        out_specs=(split, split) + (rows,) * 12 + (cols,) * 3,
        check_vma=False,
    )
```

time: 1020 us -> 717 us (0.70); the launches traced: 1010 us -> 716 us
  matrix products: 123 us -> 0 us
  local copies, waits for them, and re-layouts: 122 us -> 11.3 us
  waiting for transfers between devices: 414 us -> 304 us
  Pallas kernels: 0 us -> 96.4 us
  other arithmetic: 60.4 us -> 24.2 us
  starting transfers between devices: 14 us -> 0.25 us
    dot_general x18 -> x0, matrix products: 123 us -> none  [the longest x1 28.8 us: on_device(): jnp.dot(normed_mid_low, w_fc1, preferred_element_type=jnp.float32)]
    unnamed x9 -> x7, waiting for transfers between devices: 124 us -> 22.2 us
    pallas_call x0 -> x1, Pallas kernels: none -> 96.4 us  [run_layer(): pl.pallas_call(functools.partial(layer_kernel, stages=stages), out_shape=...]
    reshape x11 -> x1, local copies, waits for them, and re-layouts: 67.2 us -> 2.14 us  [by_pair(): weight.reshape(rows, 3, PAIRS, cols // (3 * PAIRS)).transpose(2, 0, 1, 3)]
    all_to_all x3 -> x0, local copies, waits for them, and re-layouts: 28.6 us -> none  [the longest x1 17.6 us: on_device(): lax.all_to_all(stacked, 'head', split_axis=0, concat_axis=3, tiled=True)]
    reduce_sum x11 -> x0, other arithmetic: 24.1 us -> none  [the longest x2 4.63 us: layer_norm(): return centred * lax.rsqrt(variance + norm_eps) * gain_row + shift_row]
    unnamed x1, blocking collectives: 77.2 us -> 95.2 us
    all_to_all x2 -> x0, blocking collectives: 16.1 us -> none  [the longest x1 9.54 us: on_device(): lax.all_to_all(stacked, 'head', split_axis=0, concat_axis=3, tiled=True)]
  transfers between devices with their start and end apart: 10 -> 6, of which waited for: 6 -> 4; matrix products, arithmetic and copies ran while one was open for 13% -> 3% of each run, Pallas kernels for 0% -> 0%
where the time goes in v1:
time: 717 us; the launch traced here: 716 us
  waiting for transfers between devices  304 us (42%)
  blocking collectives  265 us (37%)
  Pallas kernels  96.4 us (13%)
  other arithmetic  24.2 us (3%)
  between operations  15 us (2%)
  local copies, waits for them, and re-layouts  11.3 us (2%)
    reduce_scatter x2, waiting for transfers between devices, on_device(): lax.psum_scatter(lax.psum(g.astype(BF16), 'head').astype(F32), 'dp', scat...  262 us
    pallas_call x1, Pallas kernels, run_layer(): pl.pallas_call(functools.partial(layer_kernel, stages=stages), out_shape=...  96.4 us
    unnamed x1, blocking collectives  95.2 us
    all_gather x1, blocking collectives, on_device(): w_qkv = gather(qkv_master.astype(BF16), axis=0)  48.3 us
    all_gather x1, blocking collectives, on_device(): w_proj = gather(proj_master.astype(BF16), axis=0)  44.7 us
    psum x1, blocking collectives, on_device(): totals = lax.psum(jnp.sum(onehot * kept_rows[:, None], 0), ('dp', 'head'))  37.3 us
    all_gather x1, blocking collectives, on_device(): vectors = gather(vec_master.astype(BF16), axis=1).astype(F32)  35.8 us
    unnamed x7, waiting for transfers between devices  22.2 us
  transfers between devices with their start and end apart: 6, of which 4 were waited for; matrix products, arithmetic and copies ran while one was open for 3% of the time, Pallas kernels for 0%

profile of v1, /device:TPU:0, one launch (start us, length us, event | category | flops | bytes accessed | tf_op | source)
XLA Modules:
  0.0 716.2 jit_solution(6252770319983049051)
XLA Ops:
  7.2 0.0 all-gather.4.cloned.1.call-start
  7.2 1.6 convert_element_type.67
  8.8 0.0 all-gather.4.cloned.1.call-update
  8.8 0.0 all-gather.6.cloned.1.call-start
  8.9 1.6 convert_element_type.68
  10.4 0.0 all-gather.6.cloned.1.call-update
  10.4 0.0 all-reduce.10.cloned.1.call-start
  10.5 0.9 convert_element_type.65
  11.4 48.3 %all_gather.15 = bf16[384,1152]{1,0:T(8,128)(2,1)S(1)} all-gather(bf16[24,1152]{1,0:T(8,128)(2,1)S(1)} %convert_element_type.65), channel_id=1, replica_groups=mesh['dp'=16,'head'=2] {'dp'}, dimensions={0}, use_global_device_ids=true | all-gather | bytes 940032 | tf_op jit(solution)/shard_map/all_gather | solution.py:357
  59.7 0.8 copy.78
  60.5 0.0 copy-start.9
  60.5 0.1 copy.79
  60.6 0.0 copy-start.8
  60.7 0.0 copy-start.21
  60.7 2.1 copy.81.wq_ref
  62.8 35.8 %all-gather = bf16[16,24,12]{1,2,0:T(8,128)(2,1)S(1)} all-gather(bf16[1,24,12]{1,2,0:T(8,128)(2,1)S(1)} %convert_bitcast_fusion), channel_id=1, replica_groups=mesh['dp'=16,'head'=2] {'dp'}, dimensions={0}, use_global_device_ids=true | all-gather | bytes 9792 | tf_op jit(solution)/shard_map/all_gather | solution.py:361
  98.7 0.7 reshape.54
  99.4 0.1 convert_reduce_fusion
  99.5 0.1 select_reduce_fusion.1
  99.6 37.3 %psum.42 = f32[96]{0:T(128)S(1)} all-reduce(f32[96]{0:T(128)S(1)} %select_reduce_fusion.1), channel_id=1, replica_groups=mesh['dp'=16,'head'=2] {'dp','head'}, use_global_device_ids=true, to_apply=%region_2.0 | all-reduce | flops 96 | bytes 768 | tf_op jit(solution)/shard_map/psum | solution.py:367
  136.9 0.2 select_reduce_fusion
  137.1 0.1 broadcast_multiply_fusion
  137.2 0.6 pad.8.tw_ref
  137.8 0.6 pad.7.keep_ref
  138.4 44.7 %all_gather.16.wp_ref = bf16[384,384]{1,0:T(8,128)(2,1)} all-gather(bf16[24,384]{1,0:T(8,128)(2,1)S(1)} %convert_element_type.66), channel_id=1, replica_groups=mesh['dp'=16,'head'=2] {'dp'}, dimensions={0}, use_global_device_ids=true | all-gather | bytes 313344 | tf_op jit(solution)/shard_map/all_gather | solution.py:358
  183.1 96.4 %layer.1 = (bf16[9,198,384]{2,1,0:T(8,128)(2,1)}, f32[9,198,384]{2,1,0:T(8,128)}, f32[3,384,384]{2,1,0:T(8,128)}, f32[384,384]{1,0:T(8,128)}, f32[384,1536]{1,0:...) custom-call(bf16[9,198,384]{2,1,0:T(8,128)(2,1)} %tok_ref.1, bf16[9,198,384]{2,1,0:T(8,128)(2,1)} %cot_ref.1, ...), custom_call_target="tpu_custom_call" | custom-call | tf_op jit(solution)/shard_map/layer/pallas_call | solution.py:297
  279.5 1.6 convert_element_type.71
  281.1 2.4 copy.82
  283.4 1.0 copy.83
  284.4 3.0 convert_element_type.78
  287.4 1.2 convert_element_type.80
  288.6 0.8 convert_element_type.76
  289.4 0.0 all-reduce.10.cloned.1.call-update
  289.4 0.0 reduce-scatter.12.cloned.1.call-start
  289.4 20.1 %all-reduce.10.cloned.1.call-done = (bf16[384,1152]{0,1:T(8,128)(2,1)}, bf16[384,384]{1,0:T(8,128)(2,1)}, bf16[384,1536]{1,0:T(8,128)(2,1)}, bf16[1536,384]{1,0:T(8,128)(2,1)}) async-done(((bf16[384,1152]{0,1:T(8,128)(2,1)}, bf16[384,384]{1,0:T(8,128)(2,1)}, bf16[384,1536]{1,0:T(8,128)(2,1)}, bf16[1536,384]{1,0:T(8,128)(2,1)}), (bf16[384,1152]{0,1:T(8,128)(2,1)}, bf16[384,384]{1,0:T(8,128)(2,1)}, ...) | async-done | bytes 3538960 | tf_op jit(solution)/shard_map/psum | solution.py:377
  309.6 1.9 convert_element_type.77
  311.5 0.0 reduce-scatter.12.cloned.1.call-update
  311.6 0.0 reduce-scatter.10.cloned.1.call-start
  311.6 1.6 convert_element_type.81
  313.2 0.0 reduce-scatter.10.cloned.1.call-update
  313.2 0.0 reduce-scatter.8.cloned.1.call-start
  313.3 1.2 copy-done.1
  314.5 1.7 convert_element_type.79
  316.2 0.0 reduce-scatter.8.cloned.1.call-update
  316.2 0.6 copy-done.22
  316.8 0.6 dynamic-slice
  318.1 3.3 psum.47
  321.5 0.0 copy-start.15
  321.5 95.2 %all-reduce.11 = (f32[384,1152]{0,1:T(8,128)S(1)}, f32[12,384]{1,0:T(8,128)}) all-reduce(bf16[384,1152]{0,1:T(8,128)(2,1)S(1)} %copy-done.3, bf16[12,384]{1,0:T(8,128)(2,1)S(1)} %psum.47), channel_id=2, replica_groups=mesh['dp'=16,'head'=2] {'dp'}, use_global_device_ids=true, to_apply=%region_5.6.clone | all-reduce | flops 446976 | bytes 2681856
  416.7 0.0 copy-start.10
  416.7 0.0 copy-start.16
  416.8 0.0 copy-start.12
  416.8 0.2 constant_dynamic-slice_fusion
  417.0 0.0 copy-start.13
  417.0 0.0 copy-start.14
  417.0 0.2 copy.84
  417.2 1.4 multiply_subtract_fusion.4
  418.7 1.7 multiply_subtract_fusion.2
  420.4 22.1 %reduce-scatter.12.cloned.1.call-done = f32[24,384]{1,0:T(8,128)} async-done(((f32[384,384]{1,0:T(8,128)}), f32[24,384]{1,0:T(8,128)}) %reduce-scatter.12.cloned.1.call-update) | async-done | bytes 36880
  442.4 1.4 multiply_subtract_fusion.3
  443.9 130.7 %reduce-scatter.10.cloned.1.call-done = f32[96,384]{1,0:T(8,128)} async-done(((f32[1536,384]{1,0:T(8,128)}), f32[96,384]{1,0:T(8,128)}) %reduce-scatter.10.cloned.1.call-update) | async-done | bytes 147472 | tf_op jit(solution)/shard_map/reduce_scatter | solution.py:376
  574.5 1.7 multiply_subtract_fusion
  576.3 131.3 %reduce-scatter.8.cloned.1.call-done = f32[24,1536]{1,0:T(8,128)} async-done(((f32[384,1536]{1,0:T(8,128)}), f32[24,1536]{1,0:T(8,128)}) %reduce-scatter.8.cloned.1.call-update) | async-done | bytes 147472 | tf_op jit(solution)/shard_map/reduce_scatter | solution.py:376
  707.6 1.7 multiply_subtract_fusion.1
  (43 shorter events, 0.1 us)
Async XLA Ops:
  7.2 175.9 %all-gather.4.cloned.1.call-start = ((), (), s32[]{:S(2)}) async-start(), calls=%async_computation.3 | async-start | bytes 1253376 | tf_op jit(solution)/shard_map/all_gather | solution.py:359
  8.8 174.3 %all-gather.6.cloned.1.call-start = ((), (), s32[]{:S(2)}) async-start(), calls=%async_computation.4 | async-start | bytes 1253376 | tf_op jit(solution)/shard_map/all_gather | solution.py:360
  10.4 299.1 %all-reduce.10.cloned.1.call-start = ((), (), s32[]{:S(2)}) async-start(), calls=%async_computation.8 | async-start | bytes 7077888 | tf_op jit(solution)/shard_map/psum | solution.py:377
  60.5 2.3 copy-start.9
  60.5 2.3 copy-start.17
  60.6 38.7 %copy-start.8 = (s32[9,198]{1,0:T(8,128)S(1)}, s32[9,198]{1,0:T(8,128)}, u32[]{:S(2)}) copy-start(s32[9,198]{1,0:T(8,128)} %param.21) | copy-start | bytes 21388
  60.7 38.8 %copy-start.21 = (s32[9]{0:T(128)S(1)}, s32[9]{0:T(128)}, u32[]{:S(2)}) copy-start(s32[9]{0:T(128)} %param.22) | copy-start | bytes 112
  284.4 3.0 copy-start
  287.4 1.2 copy-start.4
  289.4 153.0 %reduce-scatter.12.cloned.1.call-start = ((), (), s32[]{:S(2)}) async-start(), calls=%async_computation.7 | async-start | bytes 626688
  309.6 2.0 copy-start.2
  311.6 263.0 %reduce-scatter.10.cloned.1.call-start = ((), (), s32[]{:S(2)}) async-start(), calls=%async_computation.6 | async-start | bytes 2506752 | tf_op jit(solution)/shard_map/reduce_scatter | solution.py:376
  313.2 1.3 copy-start.1
  313.2 394.3 %reduce-scatter.8.cloned.1.call-start = ((), (), s32[]{:S(2)}) async-start(), calls=%async_computation.5 | async-start | bytes 2506752 | tf_op jit(solution)/shard_map/reduce_scatter | solution.py:376
  316.2 0.7 copy-start.22
  316.2 1.9 copy-start.19
  316.2 5.3 copy-start.3
  321.4 95.8 %copy-start.18 = (f32[12,24]{1,0:T(8,128)S(1)}, f32[12,24]{1,0:T(8,128)}, u32[]{:S(2)}) copy-start(f32[12,24]{1,0:T(8,128)} %param.27) | copy-start | bytes 3460
  321.4 95.8 %copy-start.20 = (f32[12,24]{1,0:T(8,128)S(1)}, f32[12,24]{1,0:T(8,128)}, u32[]{:S(2)}) copy-start(f32[12,24]{1,0:T(8,128)} %param.37) | copy-start | bytes 3460
  321.4 97.2 %copy-start.7 = (f32[24,1152]{1,0:T(8,128)S(1)}, f32[24,1152]{1,0:T(8,128)}, u32[]{:S(2)}) copy-start(f32[24,1152]{1,0:T(8,128)} %param.23) | copy-start | bytes 331780
  321.5 97.2 %copy-start.15 = (f32[24,1152]{1,0:T(8,128)S(1)}, f32[24,1152]{1,0:T(8,128)}, u32[]{:S(2)}) copy-start(f32[24,1152]{1,0:T(8,128)} %param.33) | copy-start | bytes 331780
  416.7 25.7 %copy-start.10 = (f32[24,384]{1,0:T(8,128)S(1)}, f32[24,384]{1,0:T(8,128)}, u32[]{:S(2)}) copy-start(f32[24,384]{1,0:T(8,128)} %param.24) | copy-start | bytes 110596
  416.7 25.7 %copy-start.16 = (f32[24,384]{1,0:T(8,128)S(1)}, f32[24,384]{1,0:T(8,128)}, u32[]{:S(2)}) copy-start(f32[24,384]{1,0:T(8,128)} %param.34) | copy-start | bytes 110596
  416.8 157.8 %copy-start.5 = (f32[96,384]{1,0:T(8,128)S(1)}, f32[96,384]{1,0:T(8,128)}, u32[]{:S(2)}) copy-start(f32[96,384]{1,0:T(8,128)} %param.26) | copy-start | bytes 442372
  416.8 157.8 %copy-start.11 = (f32[96,384]{1,0:T(8,128)S(1)}, f32[96,384]{1,0:T(8,128)}, u32[]{:S(2)}) copy-start(f32[96,384]{1,0:T(8,128)} %param.36) | copy-start | bytes 442372
  416.8 157.8 %copy-start.12 = (f32[96,384]{1,0:T(8,128)S(1)}, f32[96,384]{1,0:T(8,128)}, u32[]{:S(2)}) copy-start(f32[96,384]{1,0:T(8,128)} %param.31) | copy-start | bytes 442372
  417.0 290.6 %copy-start.6 = (f32[24,1536]{1,0:T(8,128)S(1)}, f32[24,1536]{1,0:T(8,128)}, u32[]{:S(2)}) copy-start(f32[24,1536]{1,0:T(8,128)} %param.25) | copy-start | bytes 442372
  417.0 290.5 %copy-start.13 = (f32[24,1536]{1,0:T(8,128)S(1)}, f32[24,1536]{1,0:T(8,128)}, u32[]{:S(2)}) copy-start(f32[24,1536]{1,0:T(8,128)} %param.35) | copy-start | bytes 442372
  417.0 290.5 %copy-start.14 = (f32[24,1536]{1,0:T(8,128)S(1)}, f32[24,1536]{1,0:T(8,128)}, u32[]{:S(2)}) copy-start(f32[24,1536]{1,0:T(8,128)} %param.30) | copy-start | bytes 442372
Sparse Core Ops, SparseCore 0:
  11.4 60.7 all-gather.3
  75.6 55.2 all-gather.5
  289.5 20.0 all-reduce.9
  314.8 127.5 reduce-scatter.11
  447.2 127.2 reduce-scatter.9
  580.1 127.4 reduce-scatter.7

commit v2 on v1

v2 whole, which is shorter than its diff:
```python
import functools

import jax
import jax.numpy as jnp
from jax import lax
from jax.experimental import pallas as pl
from jax.experimental.pallas import tpu as pltpu
from jax.sharding import PartitionSpec as P

HEADS = 6
HEAD_DIM = 64
STEP = 10
PAIRS = HEADS // 2
SCALE = HEAD_DIM ** (-0.5)

norm_eps = 1e-06
step_rates = (0.1, 0.4, 0.1, 0.05, 0.5)
decays = (0.05, 0.05, 0.05, 0.05, 0.0)

UNITS = 12
PLANE = 4

F32 = jnp.float32
BF16 = jnp.bfloat16


def dot(left, right):
    return lax.dot_general(left, right, (((1,), (0,)), ((), ())), preferred_element_type=F32)


def across(left, right):
    return lax.dot_general(left, right, (((0,), (0,)), ((), ())), preferred_element_type=F32)


def against(left, right):
    return lax.dot_general(left, right, (((1,), (1,)), ((), ())), preferred_element_type=F32)


def normalise(values):
    average = jnp.mean(values, -1, keepdims=True)
    centred = values - average
    variance = jnp.mean(centred * centred, -1, keepdims=True)
    inverse = lax.rsqrt(variance + norm_eps)
    return centred * inverse, inverse


def norm_back(grad, unit, inverse, gain_row):
    scaled = grad * gain_row
    first = jnp.mean(scaled, -1, keepdims=True)
    second = jnp.mean(scaled * unit, -1, keepdims=True)
    return inverse * (scaled - first - unit * second)


def fold(values):
    rows, cols = values.shape
    return jnp.sum(values.reshape(rows // 8, 8, cols), 0)


ERF_A = (0.254829592, -0.284496736, 1.421413741, -1.453152027, 1.061405429)
ERF_C = 0.3275911 * 0.7071067811865476
LOG2E_HALF = 0.7213475204444817
INV_SQRT_2PI = 0.3989422804014327


def gelu_parts(x):
    bell = jnp.exp2(x * x * (-LOG2E_HALF))
    t = 1.0 / (1.0 + ERF_C * jnp.abs(x))
    a1, a2, a3, a4, a5 = (0.5 * a for a in ERF_A)
    tail = ((((a5 * t + a4) * t + a3) * t + a2) * t + a1) * t * bell
    cdf = jnp.where(x >= 0, 1.0 - tail, tail)
    return x * cdf, cdf + x * (bell * INV_SQRT_2PI)


def layer_kernel(linked, dp, sources, *refs):
    refs = list(refs)

    def take(count):
        taken = refs[:count]
        del refs[:count]
        return taken

    tok_hbm, cot_hbm, keep_ref = take(3)
    if linked:
        src_ref, qm_ref, pm_ref, f1_ref, f2_ref, vm_ref = take(6)
        out_hbm, gin_hbm, share_ref, vshare_ref = take(4)
        wq_ref, wp_ref, w1_ref, w2_ref, vec_ref = take(5)
        slabs, vslabs, tot_mine, tot_in, pair_in, pair_sum, plane_in, layer_out, layer_in = take(9)
        vsum, vin, share_in, send, recv = take(5)
    else:
        tw_ref, wq_ref, wp_ref, w1_ref, w2_ref, vec_ref = take(6)
        out_hbm, gin_hbm, gq_ref, gp_ref, g1_ref, g2_ref, gvec_ref = take(7)
    tok, cot, xs, normed, qkv, probs, att, middle, nmid, act, gel, gol, gml, twc, sums, acc = take(16)
    outs, gins, keepf, tws, local = take(5)

    images, length, feat = tok.shape
    padded = xs.shape[1]
    hidden_units = w1_ref.shape[1] // feat
    lane = lax.broadcasted_iota(jnp.int32, (padded, 128), 1)
    low_half = lane < HEAD_DIM

    def each_image(body, first=0, last=None):
        lax.fori_loop(first, images if last is None else last, lambda i, c: (body(i), c)[1], 0)

    def row(n):
        return vec_ref[n : n + 1, :]

    def stacked_halves(values):
        zero = jnp.zeros_like(values)
        return jnp.concatenate(
            [jnp.where(low_half, values, zero), jnp.where(low_half, zero, values)], 0
        )

    def merged_halves(values):
        return jnp.where(low_half, values[:padded], values[padded:])

    tok_in = pltpu.make_async_copy(tok_hbm, tok, local.at[0])
    cot_in = pltpu.make_async_copy(cot_hbm, cot, local.at[1])
    out_copy = pltpu.make_async_copy(outs, out_hbm, local.at[2])
    gin_copy = pltpu.make_async_copy(gins, gin_hbm, local.at[3])
    tok_in.start()
    cot_in.start()

    started = []
    if linked:
        me = lax.axis_index("dp")
        core = lax.axis_index("head")
        layers = dp // PLANE
        layer, place = me // PLANE, me % PLANE
        counter = [0]
        shard = 24

        def peers(kind):
            if kind == "layer":
                return [(((layer + r) % layers) * PLANE + place, core) for r in range(1, layers)]
            if kind == "plane":
                return [(layer * PLANE + (place + r) % PLANE, core) for r in range(1, PLANE)]
            return [(me, 1 - core)]

        def push(kind, pick):
            copies = []
            for r, device in enumerate(peers(kind), 1):
                src, dst = pick(r)
                k = counter[0]
                counter[0] += 1
                copy = pltpu.make_async_remote_copy(
                    src_ref=src,
                    dst_ref=dst,
                    send_sem=send.at[k],
                    recv_sem=recv.at[k],
                    device_id=device,
                    device_id_type=pl.DeviceIdType.MESH,
                )
                copy.start()
                copies.append(copy)
            started.extend(copies)
            return copies

        def arrive(copies):
            for copy in copies:
                copy.wait_recv()

        barrier = pltpu.get_barrier_semaphore()
        everyone = peers("layer") + peers("plane") + peers("core")
        for device in everyone:
            pl.semaphore_signal(
                barrier, inc=1, device_id=device, device_id_type=pl.DeviceIdType.MESH
            )

        def own_block(u):
            if u < PAIRS:
                parts = [qm_ref[:, n * feat + 128 * u : n * feat + 128 * u + 128] for n in range(3)]
                return jnp.concatenate(parts, 1)
            if u == 3:
                return pm_ref[...]
            if u < 8:
                return f1_ref[:, feat * (u - 4) : feat * (u - 3)]
            return f2_ref[shard * (u - 8) : shard * (u - 7), :]

        vslabs[place, layer] = jnp.zeros((16, 128), BF16)
        vslabs[place, layer, 0:12, 0:shard] = vm_ref[...].astype(BF16)
        for u, other in ((0, 1), (2, 3), (4, 6), (5, 7), (8, 10), (9, 11)):
            mine_now = u + (other - u) * core
            slabs[mine_now, place, layer] = jnp.where(
                core == 0, own_block(u), own_block(other)
            ).astype(BF16)

        kept = jnp.sum(keep_ref[...].astype(F32), 1, keepdims=True)
        width = tot_mine.shape[1]
        source_lane = lax.broadcasted_iota(jnp.int32, (1, width), 1)
        mine = jnp.zeros((1, width), F32)
        for i in range(images):
            mine = mine + jnp.where(source_lane == src_ref[i], kept[i : i + 1], 0.0)
        tot_mine[0:8] = jnp.broadcast_to(mine, (8, width))

        pl.semaphore_wait(barrier, len(everyone))

        def vec_push(kind):
            if kind == "layer":
                return push(kind, lambda r: (vslabs.at[place, layer],) * 2)
            return push(kind, lambda r: (vslabs.at[place],) * 2)

        def tot_push(kind, stage):
            part = pl.ds(8 * stage, 8)
            return push(kind, lambda r: (tot_mine.at[part], tot_in.at[3 * stage + r - 1]))

        def tot_sum(stage, count):
            total = tot_mine[8 * stage : 8 * stage + 8]
            for r in range(count):
                total = total + tot_in[3 * stage + r]
            tot_mine[8 * stage + 8 : 8 * stage + 16] = total

        def step_units(step):
            return (pl.ds(core, 1), pl.ds(2 + core, 1), pl.ds(4 + 2 * core, 2), pl.ds(8 + 2 * core, 2))[
                step
            ]

        def weights_push(step, kind):
            units = step_units(step)
            if kind == "layer":
                return push(kind, lambda r: (slabs.at[units, place, layer],) * 2)
            if kind == "plane":
                return push(kind, lambda r: (slabs.at[units, place],) * 2)
            return push(kind, lambda r: (slabs.at[units],) * 2)

        def assemble(u):
            for q in range(layers):
                for k in range(0, PLANE, 2):
                    both = jnp.concatenate(
                        [slabs[u, k, q].astype(F32), slabs[u, k + 1, q].astype(F32)], 0
                    ).astype(BF16)
                    first = shard * (PLANE * q + k)
                    rows = slice(first, first + 2 * shard)
                    if u < PAIRS:
                        wq_ref[u, rows, :] = both
                    elif u == 3:
                        wp_ref[rows, :] = both
                    else:
                        w1_ref[rows, feat * (u - 4) : feat * (u - 3)] = both

        def assemble_w2():
            for q in range(layers):
                for k in range(PLANE):
                    for j in range(0, 4, 2):
                        both = jnp.concatenate(
                            [slabs[8 + j, k, q].astype(F32), slabs[9 + j, k, q].astype(F32)], 0
                        ).astype(BF16)
                        first = 4 * shard * (PLANE * q + k) + shard * j
                        w2_ref[first : first + 2 * shard, :] = both

        def spread(values, owner):
            lanes = lax.broadcasted_iota(jnp.int32, (16, 128), 1)
            shift = (shard * owner) % 128
            moved = pltpu.roll(values, shift, 1) if shift else values
            block = shard * owner // 128
            here = jnp.where(lanes >= shift, moved, 0.0)
            vec_ref[:, 128 * block : 128 * block + 128] += here
            if shift + shard > 128:
                rest = jnp.where(lanes < shift, moved, 0.0)
                vec_ref[:, 128 * block + 128 : 128 * block + 256] += rest

        vec_go = vec_push("layer")
        go0 = weights_push(0, "layer")
        tot_go = tot_push("layer", 0)
        arrive(vec_go)
        vec_go = vec_push("plane")
        arrive(go0)
        go0 = weights_push(0, "plane")
        go1 = weights_push(1, "layer")
        arrive(tot_go)
        tot_sum(0, layers - 1)
        tot_go = tot_push("plane", 1)
        arrive(vec_go)
        vec_ref[...] = jnp.zeros_like(vec_ref)
        for owner in range(dp):
            spread(vslabs[owner % PLANE, owner // PLANE].astype(F32), owner)

    tail = padded - 16
    xs[:, tail:, :] = jnp.zeros((images, 16, feat), BF16)
    gol[:, tail:, :] = jnp.zeros((images, 16, feat), BF16)
    sums[...] = jnp.zeros_like(sums)
    keepf[...] = jnp.zeros_like(keepf)
    keepf[0:images, 0:length] = keep_ref[...].astype(F32)

    def first_norm(i):
        xs[i, 0:length, :] = tok[i]
        unit, _ = normalise(xs[i].astype(F32))
        normed[i] = (unit * row(0) + row(1)).astype(BF16)

    tok_in.wait()
    each_image(first_norm)

    if linked:
        arrive(go0)
        go0 = weights_push(0, "core")
        arrive(go1)
        go1 = weights_push(1, "plane")
        go2 = weights_push(2, "layer")
        arrive(tot_go)
        tot_sum(1, PLANE - 1)
        tot_go = tot_push("core", 2)
        arrive(go0)
        assemble(0)
        assemble(1)

    def project(h, i):
        part = pl.ds(128 * h, 128)
        bias = jnp.concatenate(
            [vec_ref[2:3, part], jnp.zeros((1, 128), F32), vec_ref[3:4, part]], 1
        )
        qkv[h, i] = (dot(normed[i], wq_ref[h]) + bias).astype(BF16)

    def attend(h, i):
        alive = keepf[pl.ds(i, 1), 0:padded] > 0
        query = stacked_halves(qkv[h, i, :, 0:128] * BF16(SCALE))
        scores = against(query, qkv[h, i, :, 128:256])
        scores = jnp.where(alive, scores, -1e9)
        top = jnp.max(scores, -1, keepdims=True)
        raised = jnp.exp(scores - top)
        share = raised * (1.0 / jnp.sum(raised, -1, keepdims=True))
        share = share.astype(BF16)
        probs[h, i] = share
        att[i, :, 128 * h : 128 * h + 128] = merged_halves(
            dot(share, qkv[h, i, :, 256:384])
        ).astype(BF16)

    for h in range(PAIRS):
        if linked and h == 1:
            arrive(go1)
            go1 = weights_push(1, "core")
            arrive(go2)
            go2 = weights_push(2, "plane")
            go3 = weights_push(3, "layer")
        if linked and h == 2:
            arrive(go1)
            assemble(2)
            assemble(3)
            arrive(go2)
            go2 = weights_push(2, "core")
            arrive(go3)
            go3 = weights_push(3, "plane")
        each_image(functools.partial(project, h))
        each_image(functools.partial(attend, h))

    if linked:
        arrive(tot_go)
        tot_sum(2, 1)
        totals = tot_mine[24:25]
        for i in range(images):
            total = jnp.sum(
                jnp.where(source_lane == src_ref[i], totals, 0.0), 1, keepdims=True
            )
            tws[i : i + 1] = keepf[i : i + 1] * (length / total)
    else:
        tws[...] = jnp.zeros_like(tws)
        tws[0:images, 0:length] = tw_ref[...]

    def second_norm(i):
        mid = xs[i].astype(F32) + (dot(att[i], wp_ref[...]) + row(4))
        middle[i] = mid
        unit, _ = normalise(mid)
        nmid[i] = (unit * row(5) + row(6)).astype(BF16)

    each_image(second_norm)
    if linked:
        arrive(go2)
        for u in range(4, 8):
            assemble(u)
        arrive(go3)
        go3 = weights_push(3, "core")

    def expand(i):
        values = nmid[i]
        for j in range(hidden_units):
            cols = slice(feat * j, feat * j + feat)
            pre = dot(values, w1_ref[:, cols]) + row(8 + j)
            active, slope = gelu_parts(pre)
            act[i, :, cols] = active.astype(BF16)
            gel[i, :, cols] = slope.astype(BF16)

    each_image(expand)
    if linked:
        arrive(go3)
        assemble_w2()

    def contract(i):
        total = middle[i] + (dot(act[i], w2_ref[...]) + row(7))
        outs[i] = total[:length].astype(BF16)

    each_image(contract)
    out_copy.start()

    eye = lax.broadcasted_iota(jnp.int32, (padded, padded), 0) == lax.broadcasted_iota(
        jnp.int32, (padded, padded), 1
    )

    def hidden_back(i):
        weight_row = tws[pl.ds(i, 1), 0:padded]
        column = jnp.sum(jnp.where(eye, weight_row, 0.0), 1, keepdims=True)
        twc[i] = jnp.broadcast_to(column, (padded, 128))
        wide = jnp.concatenate([twc[i]] * (feat // 128), 1)[:length]
        gol[i, 0:length, :] = (cot[i].astype(F32) * wide).astype(BF16)
        grad = gol[i]
        sums[7] += fold(grad.astype(F32))
        for j in range(hidden_units):
            cols = slice(feat * j, feat * j + feat)
            back = against(grad, w2_ref[cols, :]) * gel[i, :, cols].astype(F32)
            back = back.astype(BF16)
            gel[i, :, cols] = back
            sums[8 + j] += fold(back.astype(F32))

    cot_in.wait()
    each_image(hidden_back)

    acc[...] = jnp.zeros_like(acc)

    def fc2_grad(i):
        for j in range(hidden_units):
            acc[j] += across(act[i, :, feat * j : feat * j + feat], gol[i])

    each_image(fc2_grad)

    if linked:
        def job_units(job, owner):
            return (pl.ds(8 + 2 * owner, 2), pl.ds(4 + 2 * owner, 2), pl.ds(2 + owner, 1), pl.ds(owner, 1))[job]

        def job_slots(job):
            return (0, 2), (2, 4), (4, 5), (5, 6)

        job_slot = ((0, 2), (2, 4), (4, 5), (5, 6))

        def emit(u, source_block):
            for owner in range(dp):
                slabs[u, owner % PLANE, owner // PLANE] = source_block(owner).astype(BF16)

        def grads_pair(job):
            first, last = job_slot[job]
            theirs = job_units(job, 1 - core)
            return push("core", lambda r: (slabs.at[theirs], pair_in.at[pl.ds(first, last - first)]))

        def first_unit(job):
            return (8 + 2 * core, 4 + 2 * core, 2 + core, core)[job]

        def grads_plane(job):
            first, last = job_slot[job]
            for s in range(first, last):
                unit = first_unit(job) + (s - first)
                for k in range(PLANE):
                    for q in range(layers):
                        pair_sum[s, k, q] = (
                            slabs[unit, k, q].astype(F32) + pair_in[s, k, q].astype(F32)
                        ).astype(BF16)
            size = pl.ds(first, last - first)
            return push(
                "plane",
                lambda r: (pair_sum.at[size, (place + r) % PLANE], plane_in.at[r - 1, size]),
            )

        def grads_layer(job):
            first, last = job_slot[job]
            for s in range(first, last):
                for q in range(layers):
                    total = pair_sum[s, place, q].astype(F32)
                    for r in range(PLANE - 1):
                        total = total + plane_in[r, s, q].astype(F32)
                    layer_out[s, q] = total.astype(BF16)
            size = pl.ds(first, last - first)
            return push(
                "layer",
                lambda r: (layer_out.at[size, (layer + r) % layers], layer_in.at[r - 1, size]),
            )

        def grads_share(job):
            first, last = job_slot[job]
            units = job_units(job, core)
            for s in range(first, last):
                total = layer_out[s, layer].astype(F32)
                for r in range(layers - 1):
                    total = total + layer_in[r, s].astype(F32)
                share_in[first_unit(job) + (s - first)] = total
            return push("core", lambda r: (share_in.at[units], share_in.at[units]))

        for copy in started:
            copy.wait_send()
        started.clear()
        shares = []
        for j in range(4):
            emit(8 + j, lambda owner: acc[
                4 * shard * owner // feat,
                (4 * shard * owner) % feat + shard * j : (4 * shard * owner) % feat + shard * j + shard,
            ])
        jobs = [grads_pair(0)]
    else:
        for j in range(hidden_units):
            g2_ref[feat * j : feat * j + feat, :] = acc[j]

    def middle_back(i):
        unit, inverse = normalise(middle[i])
        grad = against(gel[i], w1_ref[...])
        sums[5] += fold(grad * unit)
        sums[6] += fold(grad)
        middle[i] = norm_back(grad, unit, inverse, row(5))
        wide = jnp.concatenate([twc[i]] * (feat // 128), 1)[:length]
        middle[i, 0:length, :] += cot[i].astype(F32) * wide
        low = middle[i].astype(BF16)
        gml[i] = low
        sums[4] += fold(low.astype(F32))

    each_image(middle_back)
    if linked:
        arrive(jobs[0])
        jobs[0] = grads_plane(0)

    acc[...] = jnp.zeros_like(acc)

    def fc1_grad(i):
        for j in range(hidden_units):
            acc[j] += across(nmid[i], gel[i, :, feat * j : feat * j + feat])

    each_image(fc1_grad)
    if linked:
        for j in range(4):
            emit(4 + j, lambda owner: acc[j, shard * owner : shard * owner + shard])
        jobs.append(grads_pair(1))
    else:
        for j in range(hidden_units):
            g1_ref[:, feat * j : feat * j + feat] = acc[j]

    acc[...] = jnp.zeros_like(acc)

    def proj_grad(i):
        acc[3] += across(att[i], gml[i])

    each_image(proj_grad)
    if linked:
        arrive(jobs[0])
        jobs[0] = grads_layer(0)
        arrive(jobs[1])
        jobs[1] = grads_plane(1)
        emit(3, lambda owner: acc[3, shard * owner : shard * owner + shard])
    else:
        gp_ref[...] = acc[3]

    def grad_attended(i):
        att[i] = against(gml[i], wp_ref[...]).astype(BF16)

    each_image(grad_attended)

    def attend_back(h, i):
        grad = stacked_halves(att[i, :, 128 * h : 128 * h + 128])
        key = qkv[h, i, :, 128:256]
        query = stacked_halves(qkv[h, i, :, 0:128] * BF16(SCALE))
        share_low = probs[h, i]
        share = share_low.astype(F32)
        grad_share = against(grad, qkv[h, i, :, 256:384])
        inner = jnp.sum(share * grad_share, -1, keepdims=True)
        grad_score = (share * (grad_share - inner)).astype(BF16)
        grad_query = (merged_halves(dot(grad_score, key)) * SCALE).astype(BF16)
        grad_key = across(grad_score, query).astype(BF16)
        grad_value = across(share_low, grad).astype(BF16)
        qkv[h, i, :, 0:128] = grad_query
        qkv[h, i, :, 128:256] = grad_key
        qkv[h, i, :, 256:384] = grad_value
        part = slice(128 * h, 128 * h + 128)
        sums[2, :, part] += fold(grad_query.astype(F32))
        sums[3, :, part] += fold(grad_value.astype(F32))

    def qkv_grad(h, i):
        acc[h] += across(normed[i], qkv[h, i])

    for h in reversed(range(PAIRS)):
        each_image(functools.partial(attend_back, h))
        each_image(functools.partial(qkv_grad, h))
        if linked:
            emit(h, lambda owner: acc[h, shard * owner : shard * owner + shard])
            if h == 2:
                jobs.append(grads_pair(2))
                arrive(jobs[0])
                shares.append(grads_share(0))
                arrive(jobs[1])
                jobs[1] = grads_layer(1)
            if h == 1:
                arrive(jobs[2])
                jobs[2] = grads_plane(2)
                arrive(jobs[1])
                shares.append(grads_share(1))
        else:
            gq_ref[h] = acc[h]

    def input_back(i):
        unit, inverse = normalise(xs[i].astype(F32))
        grad = against(qkv[0, i], wq_ref[0])
        for h in range(1, PAIRS):
            grad = grad + against(qkv[h, i], wq_ref[h])
        sums[0] += fold(grad * unit)
        sums[1] += fold(grad)
        total = middle[i] + norm_back(grad, unit, inverse, row(0))
        gins[i] = total[:length]

    if linked:
        jobs.append(grads_pair(3))
        arrive(jobs[2])
        jobs[2] = grads_layer(2)
        each_image(input_back, 0, images // 3)
        arrive(jobs[3])
        jobs[3] = grads_plane(3)
        each_image(input_back, images // 3, images - images // 3)
        arrive(jobs[3])
        jobs[3] = grads_layer(3)
        arrive(jobs[2])
        shares.append(grads_share(2))
        each_image(input_back, images - images // 3, images)
        gin_copy.start()
        for n in range(12):
            vsum[0, n : n + 1, :] = jnp.sum(sums[n], 0, keepdims=True)
        vsum[0, 12:16, :] = jnp.zeros((4, feat), F32)
        for stage, kind in enumerate(("core", "plane", "layer")):
            go = push(kind, lambda r: (vsum.at[stage], vin.at[3 * stage + r - 1]))
            if stage == 1:
                arrive(jobs[3])
                shares.append(grads_share(3))
            arrive(go)
            total = vsum[stage]
            for r in range(len(go)):
                total = total + vin[3 * stage + r]
            vsum[stage + 1] = total
        picked = jnp.zeros((16, 128), F32)
        for owner in range(dp):
            shift = (shard * owner) % 128
            block = shard * owner // 128
            part = vsum[3, :, 128 * block : 128 * block + 128]
            part = pltpu.roll(part, 128 - shift, 1) if shift else part
            if shift + shard > 128:
                rest = pltpu.roll(vsum[3, :, 128 * block + 128 : 128 * block + 256], 128 - shift, 1)
                lanes = lax.broadcasted_iota(jnp.int32, (16, 128), 1)
                part = jnp.where(lanes < 128 - shift, part, rest)
            picked = jnp.where(me == owner, part, picked)
        vshare_ref[...] = picked
        for go in shares:
            arrive(go)
        share_ref[...] = share_in[...]
        for copy in started:
            copy.wait_send()
    else:
        each_image(input_back)
        gin_copy.start()
        for n in range(12):
            gvec_ref[n : n + 1, :] = jnp.sum(sums[n], 0, keepdims=True)
    out_copy.wait()
    gin_copy.wait()


def layer_call(linked, dp, sources, tokens, cotangent, keep, *rest):
    images, length, feat = tokens.shape
    padded = -(-length // 16) * 16
    hidden = 4 * feat
    vmem = pl.BlockSpec(memory_space=pltpu.VMEM)
    anywhere = pl.BlockSpec(memory_space=pl.ANY)
    smem = pl.BlockSpec(memory_space=pltpu.SMEM)
    shape = jax.ShapeDtypeStruct
    outs = [shape((images, length, feat), BF16), shape((images, length, feat), F32)]
    weights = [
        pltpu.VMEM((PAIRS, feat, feat), BF16),
        pltpu.VMEM((feat, feat), BF16),
        pltpu.VMEM((feat, hidden), BF16),
        pltpu.VMEM((hidden, feat), BF16),
        pltpu.VMEM((16, feat), F32),
    ]
    if linked:
        layers = dp // PLANE
        width = -(-sources // 128) * 128
        in_specs = [anywhere, anywhere, vmem, smem] + [vmem] * 5
        outs += [shape((UNITS, 24, feat), F32), shape((16, 128), F32)]
        copies = 4 * (layers - 1 + PLANE - 1 + 1) + 2 * (layers + PLANE - 2) + 1
        copies += 4 * (1 + layers - 1 + PLANE - 1 + 1) + layers + PLANE - 1
        links = [
            pltpu.VMEM((UNITS, PLANE, layers, 24, feat), BF16),
            pltpu.VMEM((PLANE, layers, 16, 128), BF16),
            pltpu.VMEM((32, width), F32),
            pltpu.VMEM((9, 8, width), F32),
            pltpu.VMEM((UNITS // 2, PLANE, layers, 24, feat), BF16),
            pltpu.VMEM((UNITS // 2, PLANE, layers, 24, feat), BF16),
            pltpu.VMEM((PLANE - 1, UNITS // 2, layers, 24, feat), BF16),
            pltpu.VMEM((UNITS // 2, layers, 24, feat), BF16),
            pltpu.VMEM((layers - 1, UNITS // 2, 24, feat), BF16),
            pltpu.VMEM((4, 16, feat), F32),
            pltpu.VMEM((9, 16, feat), F32),
            pltpu.VMEM((UNITS, 24, feat), F32),
            pltpu.SemaphoreType.DMA((copies,)),
            pltpu.SemaphoreType.DMA((copies,)),
        ]
    else:
        in_specs = [anywhere, anywhere] + [vmem] * 7
        outs += [shape(w.shape, F32) for w in rest[1:]]
        weights, links = [], []
    params = dict(vmem_limit_bytes=64 * 1024 * 1024)
    if linked:
        params.update(collective_id=0, has_side_effects=True)
    return pl.pallas_call(
        functools.partial(layer_kernel, linked, dp, sources),
        out_shape=outs,
        in_specs=in_specs,
        out_specs=[anywhere, anywhere] + [vmem] * (len(outs) - 2),
        scratch_shapes=weights
        + links
        + [
            pltpu.VMEM((images, length, feat), BF16),
            pltpu.VMEM((images, length, feat), BF16),
            pltpu.VMEM((images, padded, feat), BF16),
            pltpu.VMEM((images, padded, feat), BF16),
            pltpu.VMEM((PAIRS, images, padded, feat), BF16),
            pltpu.VMEM((PAIRS, images, 2 * padded, padded), BF16),
            pltpu.VMEM((images, padded, feat), BF16),
            pltpu.VMEM((images, padded, feat), F32),
            pltpu.VMEM((images, padded, feat), BF16),
            pltpu.VMEM((images, padded, hidden), BF16),
            pltpu.VMEM((images, padded, hidden), BF16),
            pltpu.VMEM((images, padded, feat), BF16),
            pltpu.VMEM((images, padded, feat), BF16),
            pltpu.VMEM((images, padded, 128), F32),
            pltpu.VMEM((12, 8, feat), F32),
            pltpu.VMEM((4, feat, feat), F32),
            pltpu.VMEM((images, length, feat), BF16),
            pltpu.VMEM((images, length, feat), F32),
            pltpu.VMEM((16, 256), F32),
            pltpu.VMEM((16, 256), F32),
            pltpu.SemaphoreType.DMA((4,)),
        ],
        compiler_params=pltpu.CompilerParams(**params),
        name="layer",
    )(tokens, cotangent, keep, *rest)


def adamw(master, first, second, gradient, step_rate, weight_decay):
    first_new = 0.9 * first + 0.1 * gradient
    second_new = 0.999 * second + 0.001 * gradient * gradient
    step_size = first_new / (1.0 - 0.9**STEP) / (jnp.sqrt(second_new / (1.0 - 0.999**STEP)) + 1e-08)
    return (first_new, second_new, master - step_rate * (step_size + weight_decay * master))


def step_kernel(share_ref, vshare_ref, *refs):
    state, outs = refs[:15], refs[15:]
    feat = share_ref.shape[2]

    def update(n, here, gradient):
        new = adamw(
            state[n][here], state[5 + n][here], state[10 + n][here], gradient, step_rates[n], decays[n]
        )
        for k in range(3):
            outs[3 * n + k][here] = new[k]

    everything = slice(None)
    for u in range(PAIRS):
        for n in range(3):
            first = n * feat + 128 * u
            update(0, (everything, slice(first, first + 128)), share_ref[u, :, 128 * n : 128 * n + 128])
    update(1, (everything, everything), share_ref[3])
    for j in range(4):
        update(2, (everything, slice(feat * j, feat * j + feat)), share_ref[4 + j])
        rows = share_ref.shape[1]
        update(3, (slice(rows * j, rows * j + rows), everything), share_ref[8 + j])
    vec = state[4]
    update(4, (everything, everything), vshare_ref[0 : vec.shape[0], 0 : vec.shape[1]])


def step_call(share, vshare, states):
    vmem = pl.BlockSpec(memory_space=pltpu.VMEM)
    shape = jax.ShapeDtypeStruct
    return pl.pallas_call(
        step_kernel,
        out_shape=[shape(states[n].shape, F32) for n in range(5) for _ in range(3)],
        in_specs=[vmem] * 17,
        out_specs=[vmem] * 15,
        name="step",
    )(share, vshare, *states)


def by_pair(weight):
    rows, cols = weight.shape
    return weight.reshape(rows, 3, PAIRS, cols // (3 * PAIRS)).transpose(2, 0, 1, 3).reshape(
        PAIRS, rows, cols // PAIRS
    )


def from_pairs(grad):
    pairs, rows, cols = grad.shape
    return grad.reshape(pairs, rows, 3, cols // 3).transpose(1, 2, 0, 3).reshape(rows, pairs * cols)


def on_device(tokens, cotangent, keep_mask, source, *states):
    masters = states[:5]
    dp = lax.axis_size("dp")
    images, length, feat = tokens.shape
    sources = images * lax.axis_size("head") * dp // 3
    if dp == 16:
        layer_out, input_grad, share, vshare = layer_call(
            True, dp, sources, tokens, cotangent, keep_mask, source, *masters
        )
        return (layer_out, input_grad, *step_call(share, vshare, states))
    gather = functools.partial(lax.all_gather, axis_name="dp", tiled=True)
    low = [master.astype(BF16) for master in masters]
    w_qkv, w_proj, w_fc1, w_fc2 = (gather(w, axis=0) for w in low[:4])
    vectors = gather(low[4], axis=1).astype(F32)
    live_mask = keep_mask.astype(F32)
    kept_rows = jnp.sum(live_mask, 1)
    onehot = (source[:, None] == jnp.arange(sources, dtype=jnp.int32)[None, :]).astype(F32)
    totals = lax.psum(jnp.sum(onehot * kept_rows[:, None], 0), ("dp", "head"))
    image_total = jnp.sum(onehot * totals[None, :], 1)
    token_weight = live_mask * (length / image_total)[:, None]
    layer_out, input_grad, gq, gp, g1, g2, gvec = layer_call(
        False, dp, sources, tokens, cotangent, keep_mask,
        token_weight, by_pair(w_qkv), w_proj, w_fc1, w_fc2, vectors,
    )
    gradients = (from_pairs(gq), gp, g1, g2, gvec)
    dims = (0, 0, 0, 0, 1)
    shares = [
        lax.psum_scatter(
            lax.psum(g.astype(BF16), "head").astype(F32), "dp", scatter_dimension=d, tiled=True
        )
        for g, d in zip(gradients, dims)
    ]
    new = []
    for n in range(5):
        new.extend(
            adamw(masters[n], states[5 + n], states[10 + n], shares[n], step_rates[n], decays[n])
        )
    return (layer_out, input_grad, *new)


def solution(mesh):
    split = P(("dp", "head"), None, None)
    rows, cols = P("dp", None), P(None, "dp")
    weights = (rows, rows, rows, rows, cols)
    return jax.shard_map(
        on_device,
        mesh=mesh,
        in_specs=(split, split, P(("dp", "head"), None), P(("dp", "head"))) + weights * 3,
        out_specs=(split, split) + (rows,) * 12 + (cols,) * 3,
        check_vma=False,
    )
```

time: 717 us -> 148 us (0.21)
  waiting for transfers between devices: 304 us -> 0 us
  blocking collectives: 265 us -> 0 us
  Pallas kernels: 96.4 us -> 144 us
  other arithmetic: 24.2 us -> 0 us
  between operations: 15 us -> 0.69 us
  local copies, waits for them, and re-layouts: 11.3 us -> 3.82 us
    reduce_scatter x2 -> x0, waiting for transfers between devices: 262 us -> none  [on_device(): lax.psum_scatter(lax.psum(g.astype(BF16), 'head').astype(F32), 'dp', scat...]
    all_gather x3 -> x0, blocking collectives: 129 us -> none  [the longest x1 48.3 us: on_device(): w_qkv = gather(qkv_master.astype(BF16), axis=0)]
    unnamed x1 -> x0, blocking collectives: 95.2 us -> none
    pallas_call x1 -> x2, Pallas kernels: 96.4 us -> 144 us  [the longest x1 141 us: layer_call(): pl.pallas_call(functools.partial(layer_kernel, linked, dp, sources), out_...]
    psum x2 -> x0, blocking collectives: 40.7 us -> none  [the longest x1 37.3 us: on_device(): totals = lax.psum(jnp.sum(onehot * kept_rows[:, None], 0), ('dp', 'head'))]
    unnamed x7 -> x0, waiting for transfers between devices: 22.2 us -> none
    psum x1 -> x0, waiting for transfers between devices: 20.1 us -> none  [on_device(): lax.psum(g.astype(BF16), 'head').astype(F32)]
    convert_element_type x14 -> x0, other arithmetic: 15.8 us -> none  [the longest x5 6.5 us: on_device(): g.astype(BF16)]
  transfers between devices with their start and end apart: 6 -> 0, of which waited for: 4 -> 0; matrix products, arithmetic and copies ran while one was open for 3% -> 0% of each run, Pallas kernels for 0% -> 0%
where the time goes in v2:
time: 148 us
  Pallas kernels  144 us (97%)
  local copies, waits for them, and re-layouts  3.82 us (3%)
    pallas_call x1, Pallas kernels, layer_call(): pl.pallas_call(functools.partial(layer_kernel, linked, dp, sources), out_...  141 us
    unnamed x6, local copies, waits for them, and re-layouts  3.82 us

profile of v2, /device:TPU:0, one launch (start us, length us, event | category | flops | bytes accessed | tf_op | source)
XLA Modules:
  0.0 148.2 jit_solution(6216791622487256419)
XLA Ops:
  0.7 140.7 %layer.1 = (bf16[9,198,384]{2,1,0:T(8,128)(2,1)}, f32[9,198,384]{2,1,0:T(8,128)}, f32[12,24,384]{2,1,0:T(8,128)}, f32[16,128]{1,0:T(8,128)}) custom-call(bf16[9,198,384]{2,1,0:T(8,128)(2,1)} %refs_0_.2, bf16[9,198,384]{2,1,0:T(8,128)(2,1)} %refs_1_.2, s32[9,198]{1,0:T(8,128)} %refs_2_.2, s32[9]{0:T(128)} %refs_3_.2, f32[24,1152]{1,0:T(8,128)} %refs_0_.3, ...), custom_call_target="tpu_custom_call" | custom-call | tf_op jit(solution)/shard_map/layer/pallas_call | solution.py:698
  141.4 0.0 copy-start.1
  141.4 3.0 %step.1 = (f32[24,1152]{1,0:T(8,128)}, f32[24,1152]{1,0:T(8,128)}, f32[24,1152]{1,0:T(8,128)}, f32[24,384]{1,0:T(8,128)}, f32[24,384]{1,0:T(8,128)}, /*index=5*/...) custom-call(f32[12,24,384]{2,1,0:T(8,128)} %get-tuple-element.38.sha, ...), custom_call_target="tpu_custom_call" | custom-call | tf_op jit(solution)/shard_map/step/pallas_call | solution.py:768
  144.3 0.0 copy-done.1
  144.3 0.0 copy-start
  144.4 1.1 copy.38
  145.4 1.2 copy-done
  146.6 1.5 %copy.39 = f32[9,198,384]{2,1,0:T(8,128)} copy(f32[9,198,384]{2,1,0:T(8,128)S(1)} %copy-done) | data formatting | bytes 5474304
Async XLA Ops:
  141.4 3.0 %copy-start.1 = (bf16[9,198,384]{2,1,0:T(8,128)(2,1)S(1)}, bf16[9,198,384]{2,1,0:T(8,128)(2,1)}, u32[]{:S(2)}) copy-start(bf16[9,198,384]{2,1,0:T(8,128)(2,1)} %get-tuple-element.72) | copy-start | bytes 4105732
  144.3 2.3 %copy-start = (f32[9,198,384]{2,1,0:T(8,128)S(1)}, f32[9,198,384]{2,1,0:T(8,128)}, u32[]{:S(2)}) copy-start(f32[9,198,384]{2,1,0:T(8,128)} %get-tuple-element.73) | copy-start | bytes 8211460

commit v3 on v2

--- a/solution.py
+++ b/solution.py
@@ -56,19 +56,14 @@
     return jnp.sum(values.reshape(rows // 8, 8, cols), 0)
 
 
-ERF_A = (0.254829592, -0.284496736, 1.421413741, -1.453152027, 1.061405429)
-ERF_C = 0.3275911 * 0.7071067811865476
 LOG2E_HALF = 0.7213475204444817
 INV_SQRT_2PI = 0.3989422804014327
 
 
 def gelu_parts(x):
-    bell = jnp.exp2(x * x * (-LOG2E_HALF))
-    t = 1.0 / (1.0 + ERF_C * jnp.abs(x))
-    a1, a2, a3, a4, a5 = (0.5 * a for a in ERF_A)
-    tail = ((((a5 * t + a4) * t + a3) * t + a2) * t + a1) * t * bell
-    cdf = jnp.where(x >= 0, 1.0 - tail, tail)
-    return x * cdf, cdf + x * (bell * INV_SQRT_2PI)
+    cdf = 0.5 + 0.5 * lax.erf(x * 0.7071067811865476)
+    bell = jnp.exp2(x * x * (-LOG2E_HALF)) * INV_SQRT_2PI
+    return x * cdf, cdf + x * bell
 
 
 def layer_kernel(linked, dp, sources, *refs):
@@ -84,22 +79,36 @@
         src_ref, qm_ref, pm_ref, f1_ref, f2_ref, vm_ref = take(6)
         out_hbm, gin_hbm, share_ref, vshare_ref = take(4)
         wq_ref, wp_ref, w1_ref, w2_ref, vec_ref = take(5)
-        slabs, vslabs, tot_mine, tot_in, pair_in, pair_sum, plane_in, layer_out, layer_in = take(9)
+        slabs, vslabs, tot_mine, tot_in, pair_in, plane_in, layer_out, layer_in = take(8)
         vsum, vin, share_in, send, recv = take(5)
     else:
         tw_ref, wq_ref, wp_ref, w1_ref, w2_ref, vec_ref = take(6)
         out_hbm, gin_hbm, gq_ref, gp_ref, g1_ref, g2_ref, gvec_ref = take(7)
-    tok, cot, xs, normed, qkv, probs, att, middle, nmid, act, gel, gol, gml, twc, sums, acc = take(16)
-    outs, gins, keepf, tws, local = take(5)
-
-    images, length, feat = tok.shape
-    padded = xs.shape[1]
-    hidden_units = w1_ref.shape[1] // feat
+    cot, xs, normed, qkv, probs, att, middle, nmid, act, gel, gol, gml, dsc = take(13)
+    sums, sums1, b1, outs, gins, keepf, tws, local = take(8)
+
+    images, length, feat = cot.shape
+    padded = xs.shape[0] // images
+    hidden = act.shape[1]
+    hidden_units = hidden // feat
+    group = 3 if images % 3 == 0 else 1
+    chunk = 256
     lane = lax.broadcasted_iota(jnp.int32, (padded, 128), 1)
     low_half = lane < HEAD_DIM
 
-    def each_image(body, first=0, last=None):
-        lax.fori_loop(first, images if last is None else last, lambda i, c: (body(i), c)[1], 0)
+    def image_rows(i):
+        return pl.ds(pl.multiple_of(i * padded, padded), padded)
+
+    def real_rows(i):
+        return pl.ds(pl.multiple_of(i * padded, padded), length)
+
+    def each_block(body, first=0, last=None):
+        def step(t, carry):
+            rows = pl.ds(pl.multiple_of(t * group * padded, padded), group * padded)
+            body(rows, [t * group + k for k in range(group)])
+            return carry
+
+        lax.fori_loop(first, images // group if last is None else last, step, 0)
 
     def row(n):
         return vec_ref[n : n + 1, :]
@@ -113,7 +122,7 @@
     def merged_halves(values):
         return jnp.where(low_half, values[:padded], values[padded:])
 
-    tok_in = pltpu.make_async_copy(tok_hbm, tok, local.at[0])
+    tok_in = pltpu.make_async_copy(tok_hbm, outs, local.at[0])
     cot_in = pltpu.make_async_copy(cot_hbm, cot, local.at[1])
     out_copy = pltpu.make_async_copy(outs, out_hbm, local.at[2])
     gin_copy = pltpu.make_async_copy(gins, gin_hbm, local.at[3])
@@ -231,7 +240,7 @@
                     first = shard * (PLANE * q + k)
                     rows = slice(first, first + 2 * shard)
                     if u < PAIRS:
-                        wq_ref[u, rows, :] = both
+                        wq_ref[rows, feat * u : feat * u + feat] = both
                     elif u == 3:
                         wp_ref[rows, :] = both
                     else:
@@ -274,20 +283,25 @@
         for owner in range(dp):
             spread(vslabs[owner % PLANE, owner // PLANE].astype(F32), owner)
 
-    tail = padded - 16
-    xs[:, tail:, :] = jnp.zeros((images, 16, feat), BF16)
-    gol[:, tail:, :] = jnp.zeros((images, 16, feat), BF16)
+    for i in range(images):
+        tail = slice(padded * (i + 1) - 16, padded * (i + 1))
+        xs[tail, :] = jnp.zeros((16, feat), BF16)
+        gol[tail, :] = jnp.zeros((16, feat), BF16)
     sums[...] = jnp.zeros_like(sums)
+    sums1[...] = jnp.zeros_like(sums1)
     keepf[...] = jnp.zeros_like(keepf)
     keepf[0:images, 0:length] = keep_ref[...].astype(F32)
-
-    def first_norm(i):
-        xs[i, 0:length, :] = tok[i]
-        unit, _ = normalise(xs[i].astype(F32))
-        normed[i] = (unit * row(0) + row(1)).astype(BF16)
+    for j in range(hidden_units):
+        b1[0:1, feat * j : feat * j + feat] = row(8 + j)
+
+    def first_norm(_, block):
+        for i in block:
+            xs[real_rows(i), :] = outs[i]
+            unit, _ = normalise(xs[image_rows(i), :].astype(F32))
+            normed[image_rows(i), :] = (unit * row(0) + row(1)).astype(BF16)
 
     tok_in.wait()
-    each_image(first_norm)
+    each_block(first_norm)
 
     if linked:
         arrive(go0)
@@ -302,44 +316,57 @@
         assemble(0)
         assemble(1)
 
-    def project(h, i):
-        part = pl.ds(128 * h, 128)
-        bias = jnp.concatenate(
-            [vec_ref[2:3, part], jnp.zeros((1, 128), F32), vec_ref[3:4, part]], 1
-        )
-        qkv[h, i] = (dot(normed[i], wq_ref[h]) + bias).astype(BF16)
-
-    def attend(h, i):
-        alive = keepf[pl.ds(i, 1), 0:padded] > 0
-        query = stacked_halves(qkv[h, i, :, 0:128] * BF16(SCALE))
-        scores = against(query, qkv[h, i, :, 128:256])
-        scores = jnp.where(alive, scores, -1e9)
-        top = jnp.max(scores, -1, keepdims=True)
-        raised = jnp.exp(scores - top)
-        share = raised * (1.0 / jnp.sum(raised, -1, keepdims=True))
-        share = share.astype(BF16)
-        probs[h, i] = share
-        att[i, :, 128 * h : 128 * h + 128] = merged_halves(
-            dot(share, qkv[h, i, :, 256:384])
-        ).astype(BF16)
-
-    for h in range(PAIRS):
-        if linked and h == 1:
-            arrive(go1)
-            go1 = weights_push(1, "core")
-            arrive(go2)
-            go2 = weights_push(2, "plane")
-            go3 = weights_push(3, "layer")
-        if linked and h == 2:
-            arrive(go1)
-            assemble(2)
-            assemble(3)
-            arrive(go2)
-            go2 = weights_push(2, "core")
-            arrive(go3)
-            go3 = weights_push(3, "plane")
-        each_image(functools.partial(project, h))
-        each_image(functools.partial(attend, h))
+    def project(first, last):
+        cols = slice(feat * first, feat * last)
+        parts = []
+        for h in range(first, last):
+            part = pl.ds(128 * h, 128)
+            parts += [vec_ref[2:3, part], jnp.zeros((1, 128), F32), vec_ref[3:4, part]]
+        bias = jnp.concatenate(parts, 1)
+
+        def body(rows, _):
+            qkv[rows, cols] = (dot(normed[rows, :], wq_ref[:, cols]) + bias).astype(BF16)
+
+        each_block(body)
+
+    def attend(h):
+        first = feat * h
+        results = []
+        for i in range(images):
+            rows = image_rows(i)
+            alive = keepf[i : i + 1, 0:padded] > 0
+            query = stacked_halves(qkv[rows, first : first + 128] * BF16(SCALE))
+            scores = against(query, qkv[rows, first + 128 : first + 256])
+            scores = jnp.where(alive, scores, -1e9)
+            top = jnp.max(scores, -1, keepdims=True)
+            raised = jnp.exp(scores - top)
+            share = raised * (1.0 / jnp.sum(raised, -1, keepdims=True))
+            share = share.astype(BF16)
+            mixed = dot(share, qkv[rows, first + 256 : first + 384])
+            results.append((share, merged_halves(mixed).astype(BF16)))
+        for i, (share, mixed) in enumerate(results):
+            probs[h, i] = share
+            att[image_rows(i), 128 * h : 128 * h + 128] = mixed
+
+    project(0, 2)
+    attend(0)
+    if linked:
+        arrive(go1)
+        go1 = weights_push(1, "core")
+        arrive(go2)
+        go2 = weights_push(2, "plane")
+        go3 = weights_push(3, "layer")
+    attend(1)
+    if linked:
+        arrive(go1)
+        assemble(2)
+        assemble(3)
+        arrive(go2)
+        go2 = weights_push(2, "core")
+        arrive(go3)
+        go3 = weights_push(3, "plane")
+    project(2, 3)
+    attend(2)
 
     if linked:
         arrive(tot_go)
@@ -354,13 +381,13 @@
         tws[...] = jnp.zeros_like(tws)
         tws[0:images, 0:length] = tw_ref[...]
 
-    def second_norm(i):
-        mid = xs[i].astype(F32) + (dot(att[i], wp_ref[...]) + row(4))
-        middle[i] = mid
-        unit, _ = normalise(mid)
-        nmid[i] = (unit * row(5) + row(6)).astype(BF16)
-
-    each_image(second_norm)
+    def second_norm(rows, block):
+        middle[rows, :] = xs[rows, :].astype(F32) + (dot(att[rows, :], wp_ref[...]) + row(4))
+        for i in block:
+            unit, _ = normalise(middle[image_rows(i), :])
+            nmid[image_rows(i), :] = (unit * row(5) + row(6)).astype(BF16)
+
+    each_block(second_norm)
     if linked:
         arrive(go2)
         for u in range(4, 8):
@@ -368,56 +395,52 @@
         arrive(go3)
         go3 = weights_push(3, "core")
 
-    def expand(i):
-        values = nmid[i]
-        for j in range(hidden_units):
-            cols = slice(feat * j, feat * j + feat)
-            pre = dot(values, w1_ref[:, cols]) + row(8 + j)
-            active, slope = gelu_parts(pre)
-            act[i, :, cols] = active.astype(BF16)
-            gel[i, :, cols] = slope.astype(BF16)
-
-    each_image(expand)
+    def expand(rows, _):
+        values = nmid[rows, :]
+        for j in range(hidden // chunk):
+            cols = slice(chunk * j, chunk * j + chunk)
+            active, slope = gelu_parts(dot(values, w1_ref[:, cols]) + b1[0:1, cols])
+            act[rows, cols] = active.astype(BF16)
+            gel[rows, cols] = slope.astype(BF16)
+
+    each_block(expand)
     if linked:
         arrive(go3)
         assemble_w2()
 
-    def contract(i):
-        total = middle[i] + (dot(act[i], w2_ref[...]) + row(7))
-        outs[i] = total[:length].astype(BF16)
-
-    each_image(contract)
+    def contract(rows, block):
+        total = middle[rows, :] + (dot(act[rows, :], w2_ref[...]) + row(7))
+        for k, i in enumerate(block):
+            outs[i] = total[padded * k : padded * k + length].astype(BF16)
+
+    each_block(contract)
     out_copy.start()
 
     eye = lax.broadcasted_iota(jnp.int32, (padded, padded), 0) == lax.broadcasted_iota(
         jnp.int32, (padded, padded), 1
     )
 
-    def hidden_back(i):
-        weight_row = tws[pl.ds(i, 1), 0:padded]
-        column = jnp.sum(jnp.where(eye, weight_row, 0.0), 1, keepdims=True)
-        twc[i] = jnp.broadcast_to(column, (padded, 128))
-        wide = jnp.concatenate([twc[i]] * (feat // 128), 1)[:length]
-        gol[i, 0:length, :] = (cot[i].astype(F32) * wide).astype(BF16)
-        grad = gol[i]
+    def weigh(_, block):
+        for i in block:
+            weight_row = tws[pl.ds(i, 1), 0:padded]
+            column = jnp.sum(jnp.where(eye, weight_row, 0.0), 1, keepdims=True)
+            grad = cot[i].astype(F32) * column[:length]
+            gins[i] = grad
+            gol[real_rows(i), :] = grad.astype(BF16)
+
+    def hidden_back(rows, _):
+        grad = gol[rows, :]
         sums[7] += fold(grad.astype(F32))
-        for j in range(hidden_units):
-            cols = slice(feat * j, feat * j + feat)
-            back = against(grad, w2_ref[cols, :]) * gel[i, :, cols].astype(F32)
+        for j in range(hidden // chunk):
+            cols = slice(chunk * j, chunk * j + chunk)
+            back = against(grad, w2_ref[cols, :]) * gel[rows, cols].astype(F32)
             back = back.astype(BF16)
-            gel[i, :, cols] = back
-            sums[8 + j] += fold(back.astype(F32))
+            gel[rows, cols] = back
+            sums1[:, cols] += fold(back.astype(F32))
 
     cot_in.wait()
-    each_image(hidden_back)
-
-    acc[...] = jnp.zeros_like(acc)
-
-    def fc2_grad(i):
-        for j in range(hidden_units):
-            acc[j] += across(act[i, :, feat * j : feat * j + feat], gol[i])
-
-    each_image(fc2_grad)
+    each_block(weigh)
+    each_block(hidden_back)
 
     if linked:
         def job_units(job, owner):
@@ -428,9 +451,11 @@
 
         job_slot = ((0, 2), (2, 4), (4, 5), (5, 6))
 
-        def emit(u, source_block):
+        def emit(u, grad):
             for owner in range(dp):
-                slabs[u, owner % PLANE, owner // PLANE] = source_block(owner).astype(BF16)
+                slabs[u, owner % PLANE, owner // PLANE] = grad[
+                    shard * owner : shard * owner + shard
+                ].astype(BF16)
 
         def grads_pair(job):
             first, last = job_slot[job]
@@ -446,20 +471,21 @@
                 unit = first_unit(job) + (s - first)
                 for k in range(PLANE):
                     for q in range(layers):
-                        pair_sum[s, k, q] = (
+                        slabs[unit, k, q] = (
                             slabs[unit, k, q].astype(F32) + pair_in[s, k, q].astype(F32)
                         ).astype(BF16)
             size = pl.ds(first, last - first)
+            units = job_units(job, core)
             return push(
                 "plane",
-                lambda r: (pair_sum.at[size, (place + r) % PLANE], plane_in.at[r - 1, size]),
+                lambda r: (slabs.at[units, (place + r) % PLANE], plane_in.at[r - 1, size]),
             )
 
         def grads_layer(job):
             first, last = job_slot[job]
             for s in range(first, last):
                 for q in range(layers):
-                    total = pair_sum[s, place, q].astype(F32)
+                    total = slabs[first_unit(job) + (s - first), place, q].astype(F32)
                     for r in range(PLANE - 1):
                         total = total + plane_in[r, s, q].astype(F32)
                     layer_out[s, q] = total.astype(BF16)
@@ -483,135 +509,157 @@
             copy.wait_send()
         started.clear()
         shares = []
-        for j in range(4):
-            emit(8 + j, lambda owner: acc[
-                4 * shard * owner // feat,
-                (4 * shard * owner) % feat + shard * j : (4 * shard * owner) % feat + shard * j + shard,
-            ])
+
+    half = hidden // 2
+    for n in range(2):
+        grad = across(act[:, half * n : half * n + half], gol[...])
+        if linked:
+            block = 4 * shard
+            for k in range(dp // 2):
+                owner = n * dp // 2 + k
+                for j in range(4):
+                    first = block * k + shard * j
+                    slabs[8 + j, owner % PLANE, owner // PLANE] = grad[
+                        first : first + shard
+                    ].astype(BF16)
+        else:
+            g2_ref[half * n : half * n + half, :] = grad
+    if linked:
         jobs = [grads_pair(0)]
-    else:
-        for j in range(hidden_units):
-            g2_ref[feat * j : feat * j + feat, :] = acc[j]
-
-    def middle_back(i):
-        unit, inverse = normalise(middle[i])
-        grad = against(gel[i], w1_ref[...])
-        sums[5] += fold(grad * unit)
-        sums[6] += fold(grad)
-        middle[i] = norm_back(grad, unit, inverse, row(5))
-        wide = jnp.concatenate([twc[i]] * (feat // 128), 1)[:length]
-        middle[i, 0:length, :] += cot[i].astype(F32) * wide
-        low = middle[i].astype(BF16)
-        gml[i] = low
-        sums[4] += fold(low.astype(F32))
-
-    each_image(middle_back)
+
+    def middle_back(rows, block):
+        grads = against(gel[rows, :], w1_ref[...])
+        for k, i in enumerate(block):
+            here = image_rows(i)
+            grad = grads[padded * k : padded * k + padded]
+            unit, inverse = normalise(middle[here, :])
+            sums[5] += fold(grad * unit)
+            sums[6] += fold(grad)
+            middle[here, :] = norm_back(grad, unit, inverse, row(5))
+            middle[real_rows(i), :] += gins[i]
+            low = middle[here, :].astype(BF16)
+            gml[here, :] = low
+            sums[4] += fold(low.astype(F32))
+
+    each_block(middle_back)
     if linked:
         arrive(jobs[0])
         jobs[0] = grads_plane(0)
 
-    acc[...] = jnp.zeros_like(acc)
-
-    def fc1_grad(i):
-        for j in range(hidden_units):
-            acc[j] += across(nmid[i], gel[i, :, feat * j : feat * j + feat])
-
-    each_image(fc1_grad)
-    if linked:
-        for j in range(4):
-            emit(4 + j, lambda owner: acc[j, shard * owner : shard * owner + shard])
+    for n in range(2):
+        grad = across(nmid[...], gel[:, half * n : half * n + half])
+        if linked:
+            emit(4 + 2 * n, grad[:, 0:feat])
+            emit(5 + 2 * n, grad[:, feat:])
+        else:
+            g1_ref[:, half * n : half * n + half] = grad
+    if linked:
         jobs.append(grads_pair(1))
-    else:
-        for j in range(hidden_units):
-            g1_ref[:, feat * j : feat * j + feat] = acc[j]
-
-    acc[...] = jnp.zeros_like(acc)
-
-    def proj_grad(i):
-        acc[3] += across(att[i], gml[i])
-
-    each_image(proj_grad)
-    if linked:
+
+    grad = across(att[...], gml[...])
+    if linked:
+        emit(3, grad)
         arrive(jobs[0])
         jobs[0] = grads_layer(0)
         arrive(jobs[1])
         jobs[1] = grads_plane(1)
-        emit(3, lambda owner: acc[3, shard * owner : shard * owner + shard])
     else:
-        gp_ref[...] = acc[3]
-
-    def grad_attended(i):
-        att[i] = against(gml[i], wp_ref[...]).astype(BF16)
-
-    each_image(grad_attended)
-
-    def attend_back(h, i):
-        grad = stacked_halves(att[i, :, 128 * h : 128 * h + 128])
-        key = qkv[h, i, :, 128:256]
-        query = stacked_halves(qkv[h, i, :, 0:128] * BF16(SCALE))
-        share_low = probs[h, i]
-        share = share_low.astype(F32)
-        grad_share = against(grad, qkv[h, i, :, 256:384])
-        inner = jnp.sum(share * grad_share, -1, keepdims=True)
-        grad_score = (share * (grad_share - inner)).astype(BF16)
-        grad_query = (merged_halves(dot(grad_score, key)) * SCALE).astype(BF16)
-        grad_key = across(grad_score, query).astype(BF16)
-        grad_value = across(share_low, grad).astype(BF16)
-        qkv[h, i, :, 0:128] = grad_query
-        qkv[h, i, :, 128:256] = grad_key
-        qkv[h, i, :, 256:384] = grad_value
-        part = slice(128 * h, 128 * h + 128)
-        sums[2, :, part] += fold(grad_query.astype(F32))
-        sums[3, :, part] += fold(grad_value.astype(F32))
-
-    def qkv_grad(h, i):
-        acc[h] += across(normed[i], qkv[h, i])
-
-    for h in reversed(range(PAIRS)):
-        each_image(functools.partial(attend_back, h))
-        each_image(functools.partial(qkv_grad, h))
-        if linked:
-            emit(h, lambda owner: acc[h, shard * owner : shard * owner + shard])
-            if h == 2:
-                jobs.append(grads_pair(2))
-                arrive(jobs[0])
-                shares.append(grads_share(0))
-                arrive(jobs[1])
-                jobs[1] = grads_layer(1)
-            if h == 1:
-                arrive(jobs[2])
-                jobs[2] = grads_plane(2)
-                arrive(jobs[1])
-                shares.append(grads_share(1))
-        else:
-            gq_ref[h] = acc[h]
-
-    def input_back(i):
-        unit, inverse = normalise(xs[i].astype(F32))
-        grad = against(qkv[0, i], wq_ref[0])
-        for h in range(1, PAIRS):
-            grad = grad + against(qkv[h, i], wq_ref[h])
-        sums[0] += fold(grad * unit)
-        sums[1] += fold(grad)
-        total = middle[i] + norm_back(grad, unit, inverse, row(0))
-        gins[i] = total[:length]
-
+        gp_ref[...] = grad
+
+    def grad_attended(rows, _):
+        att[rows, :] = against(gml[rows, :], wp_ref[...]).astype(BF16)
+
+    each_block(grad_attended)
+
+    def attend_back(h):
+        first = feat * h
+        results = []
+        for i in range(images):
+            rows = image_rows(i)
+            grad = stacked_halves(att[rows, 128 * h : 128 * h + 128])
+            share = probs[h, i].astype(F32)
+            grad_share = against(grad, qkv[rows, first + 256 : first + 384])
+            inner = jnp.sum(share * grad_share, -1, keepdims=True)
+            grad_score = (share * (grad_share - inner)).astype(BF16)
+            key = qkv[rows, first + 128 : first + 256]
+            grad_query = (merged_halves(dot(grad_score, key)) * SCALE).astype(BF16)
+            results.append((grad_score, grad_query))
+        for i, (grad_score, _) in enumerate(results):
+            dsc[i] = grad_score
+        results = [grad_query for _, grad_query in results]
+        for i in range(images):
+            rows = image_rows(i)
+            query = stacked_halves(qkv[rows, first : first + 128] * BF16(SCALE))
+            grad = stacked_halves(att[rows, 128 * h : 128 * h + 128])
+            qkv[rows, first + 128 : first + 256] = across(dsc[i], query).astype(BF16)
+            qkv[rows, first + 256 : first + 384] = across(probs[h, i], grad).astype(BF16)
+            qkv[rows, first : first + 128] = results[i]
+
+    def qkv_grad(first, last):
+        cols = slice(feat * first, feat * last)
+        grad = across(normed[...], qkv[:, cols])
+        for h in range(first, last):
+            part = grad[:, feat * (h - first) : feat * (h - first + 1)]
+            if linked:
+                emit(h, part)
+            else:
+                gq_ref[:, feat * h : feat * h + feat] = part
+
+    attend_back(2)
+    qkv_grad(2, 3)
+    if linked:
+        jobs.append(grads_pair(2))
+        arrive(jobs[0])
+        shares.append(grads_share(0))
+        arrive(jobs[1])
+        jobs[1] = grads_layer(1)
+    attend_back(1)
+    if linked:
+        arrive(jobs[2])
+        jobs[2] = grads_plane(2)
+        arrive(jobs[1])
+        shares.append(grads_share(1))
+    attend_back(0)
+    qkv_grad(0, 2)
+
+    def input_back(rows, block):
+        moved = qkv[rows, :]
+        folded = fold(moved.astype(F32))
+        for h in range(PAIRS):
+            part = slice(128 * h, 128 * h + 128)
+            sums[2, :, part] += folded[:, feat * h : feat * h + 128]
+            sums[3, :, part] += folded[:, feat * h + 256 : feat * h + 384]
+        grads = against(moved, wq_ref[...])
+        for k, i in enumerate(block):
+            here = image_rows(i)
+            grad = grads[padded * k : padded * k + padded]
+            unit, inverse = normalise(xs[here, :].astype(F32))
+            sums[0] += fold(grad * unit)
+            sums[1] += fold(grad)
+            total = middle[here, :] + norm_back(grad, unit, inverse, row(0))
+            gins[i] = total[:length]
+
+    blocks = images // group
     if linked:
         jobs.append(grads_pair(3))
         arrive(jobs[2])
         jobs[2] = grads_layer(2)
-        each_image(input_back, 0, images // 3)
+        each_block(input_back, 0, 1)
         arrive(jobs[3])
         jobs[3] = grads_plane(3)
-        each_image(input_back, images // 3, images - images // 3)
+        each_block(input_back, 1, blocks - 1)
         arrive(jobs[3])
         jobs[3] = grads_layer(3)
         arrive(jobs[2])
         shares.append(grads_share(2))
-        each_image(input_back, images - images // 3, images)
+        each_block(input_back, blocks - 1, blocks)
         gin_copy.start()
-        for n in range(12):
+        for n in range(8):
             vsum[0, n : n + 1, :] = jnp.sum(sums[n], 0, keepdims=True)
+        for j in range(hidden_units):
+            vsum[0, 8 + j : 9 + j, :] = jnp.sum(
+                sums1[:, feat * j : feat * j + feat], 0, keepdims=True
+            )
         vsum[0, 12:16, :] = jnp.zeros((4, feat), F32)
         for stage, kind in enumerate(("core", "plane", "layer")):
             go = push(kind, lambda r: (vsum.at[stage], vin.at[3 * stage + r - 1]))
@@ -641,10 +689,14 @@
         for copy in started:
             copy.wait_send()
     else:
-        each_image(input_back)
+        each_block(input_back)
         gin_copy.start()
-        for n in range(12):
+        for n in range(8):
             gvec_ref[n : n + 1, :] = jnp.sum(sums[n], 0, keepdims=True)
+        for j in range(hidden_units):
+            gvec_ref[8 + j : 9 + j, :] = jnp.sum(
+                sums1[:, feat * j : feat * j + feat], 0, keepdims=True
+            )
     out_copy.wait()
     gin_copy.wait()
 
@@ -653,13 +705,14 @@
     images, length, feat = tokens.shape
     padded = -(-length // 16) * 16
     hidden = 4 * feat
+    rows = images * padded
     vmem = pl.BlockSpec(memory_space=pltpu.VMEM)
     anywhere = pl.BlockSpec(memory_space=pl.ANY)
     smem = pl.BlockSpec(memory_space=pltpu.SMEM)
     shape = jax.ShapeDtypeStruct
     outs = [shape((images, length, feat), BF16), shape((images, length, feat), F32)]
     weights = [
-        pltpu.VMEM((PAIRS, feat, feat), BF16),
+        pltpu.VMEM((feat, PAIRS * feat), BF16),
         pltpu.VMEM((feat, feat), BF16),
         pltpu.VMEM((feat, hidden), BF16),
         pltpu.VMEM((hidden, feat), BF16),
@@ -677,7 +730,6 @@
             pltpu.VMEM((PLANE, layers, 16, 128), BF16),
             pltpu.VMEM((32, width), F32),
             pltpu.VMEM((9, 8, width), F32),
-            pltpu.VMEM((UNITS // 2, PLANE, layers, 24, feat), BF16),
             pltpu.VMEM((UNITS // 2, PLANE, layers, 24, feat), BF16),
             pltpu.VMEM((PLANE - 1, UNITS // 2, layers, 24, feat), BF16),
             pltpu.VMEM((UNITS // 2, layers, 24, feat), BF16),
@@ -704,21 +756,21 @@
         + links
         + [
             pltpu.VMEM((images, length, feat), BF16),
-            pltpu.VMEM((images, length, feat), BF16),
-            pltpu.VMEM((images, padded, feat), BF16),
-            pltpu.VMEM((images, padded, feat), BF16),
-            pltpu.VMEM((PAIRS, images, padded, feat), BF16),
+            pltpu.VMEM((rows, feat), BF16),
+            pltpu.VMEM((rows, feat), BF16),
+            pltpu.VMEM((rows, PAIRS * feat), BF16),
             pltpu.VMEM((PAIRS, images, 2 * padded, padded), BF16),
-            pltpu.VMEM((images, padded, feat), BF16),
-            pltpu.VMEM((images, padded, feat), F32),
-            pltpu.VMEM((images, padded, feat), BF16),
-            pltpu.VMEM((images, padded, hidden), BF16),
-            pltpu.VMEM((images, padded, hidden), BF16),
-            pltpu.VMEM((images, padded, feat), BF16),
-            pltpu.VMEM((images, padded, feat), BF16),
-            pltpu.VMEM((images, padded, 128), F32),
-            pltpu.VMEM((12, 8, feat), F32),
-            pltpu.VMEM((4, feat, feat), F32),
+            pltpu.VMEM((rows, feat), BF16),
+            pltpu.VMEM((rows, feat), F32),
+            pltpu.VMEM((rows, feat), BF16),
+            pltpu.VMEM((rows, hidden), BF16),
+            pltpu.VMEM((rows, hidden), BF16),
+            pltpu.VMEM((rows, feat), BF16),
+            pltpu.VMEM((rows, feat), BF16),
+            pltpu.VMEM((images, 2 * padded, padded), BF16),
+            pltpu.VMEM((8, 8, feat), F32),
+            pltpu.VMEM((8, hidden), F32),
+            pltpu.VMEM((8, hidden), F32),
             pltpu.VMEM((images, length, feat), BF16),
             pltpu.VMEM((images, length, feat), F32),
             pltpu.VMEM((16, 256), F32),
@@ -776,14 +828,12 @@
 
 def by_pair(weight):
     rows, cols = weight.shape
-    return weight.reshape(rows, 3, PAIRS, cols // (3 * PAIRS)).transpose(2, 0, 1, 3).reshape(
-        PAIRS, rows, cols // PAIRS
-    )
+    return weight.reshape(rows, 3, PAIRS, 128).transpose(0, 2, 1, 3).reshape(rows, cols)
 
 
 def from_pairs(grad):
-    pairs, rows, cols = grad.shape
-    return grad.reshape(pairs, rows, 3, cols // 3).transpose(1, 2, 0, 3).reshape(rows, pairs * cols)
+    rows, cols = grad.shape
+    return grad.reshape(rows, PAIRS, 3, 128).transpose(0, 2, 1, 3).reshape(rows, cols)
 
 
 def on_device(tokens, cotangent, keep_mask, source, *states):

time: 148 us -> 114 us (0.77)
  Pallas kernels: 144 us -> 109 us
    pallas_call x1, Pallas kernels: 141 us -> 106 us  [layer_call(): pl.pallas_call(functools.partial(layer_kernel, linked, dp, sources), out_...]
where the time goes in v3:
time: 114 us
  Pallas kernels  109 us (96%)
  local copies, waits for them, and re-layouts  3.82 us (3%)
    pallas_call x1, Pallas kernels, layer_call(): pl.pallas_call(functools.partial(layer_kernel, linked, dp, sources), out_...  106 us
    unnamed x6, local copies, waits for them, and re-layouts  3.82 us
    pallas_call x1, Pallas kernels, step_call(): pl.pallas_call(step_kernel, out_shape=[shape(states[n].shape, F32) for n...  2.95 us

profile of v3, /device:TPU:0, one launch (start us, length us, event | category | flops | bytes accessed | tf_op | source)
XLA Modules:
  0.0 113.5 jit_solution(13971384317804410961)
XLA Ops:
  0.7 106.1 %layer.1 = (bf16[9,198,384]{2,1,0:T(8,128)(2,1)}, f32[9,198,384]{2,1,0:T(8,128)}, f32[12,24,384]{2,1,0:T(8,128)}, f32[16,128]{1,0:T(8,128)}) custom-call(bf16[9,198,384]{2,1,0:T(8,128)(2,1)} %refs_0_.2, bf16[9,198,384]{2,1,0:T(8,128)(2,1)} %refs_1_.2, s32[9,198]{1,0:T(8,128)} %refs_2_.2, s32[9]{0:T(128)} %refs_3_.2, f32[24,1152]{1,0:T(8,128)} %refs_0_.3, ...), custom_call_target="tpu_custom_call" | custom-call | tf_op jit(solution)/shard_map/layer/pallas_call | solution.py:750
  106.7 0.0 copy-start.1
  106.7 3.0 %step.1 = (f32[24,1152]{1,0:T(8,128)}, f32[24,1152]{1,0:T(8,128)}, f32[24,1152]{1,0:T(8,128)}, f32[24,384]{1,0:T(8,128)}, f32[24,384]{1,0:T(8,128)}, /*index=5*/...) custom-call(f32[12,24,384]{2,1,0:T(8,128)} %get-tuple-element.38.sha, ...), custom_call_target="tpu_custom_call" | custom-call | tf_op jit(solution)/shard_map/step/pallas_call | solution.py:820
  109.7 0.0 copy-done.1
  109.7 0.0 copy-start
  109.7 1.1 copy.38
  110.8 1.2 %copy-done = f32[9,198,384]{2,1,0:T(8,128)S(1)} copy-done((f32[9,198,384]{2,1,0:T(8,128)S(1)}, f32[9,198,384]{2,1,0:T(8,128)}, u32[]{:S(2)}) %copy-start) | copy-done | bytes 2737176
  112.0 1.5 %copy.39 = f32[9,198,384]{2,1,0:T(8,128)} copy(f32[9,198,384]{2,1,0:T(8,128)S(1)} %copy-done) | data formatting | bytes 5474304
Async XLA Ops:
  106.7 3.0 %copy-start.1 = (bf16[9,198,384]{2,1,0:T(8,128)(2,1)S(1)}, bf16[9,198,384]{2,1,0:T(8,128)(2,1)}, u32[]{:S(2)}) copy-start(bf16[9,198,384]{2,1,0:T(8,128)(2,1)} %get-tuple-element.72) | copy-start | bytes 4105732
  109.7 2.3 %copy-start = (f32[9,198,384]{2,1,0:T(8,128)S(1)}, f32[9,198,384]{2,1,0:T(8,128)}, u32[]{:S(2)}) copy-start(f32[9,198,384]{2,1,0:T(8,128)} %get-tuple-element.73) | copy-start | bytes 8211460
